TPU v7x, 128 devices: a whole 4x4x4 slice. The times are simulated.
128 devices in a mesh: attn: 8 (over x, z_hi), grp: 2 (over z_lo), tp: 8 (over y, core).
Axes of the slice: x: 4, y: 4, z: 4 (z_hi: 2, z_lo: 2; z = z_hi * 2 + z_lo), core: 2. Of those that a mesh axis runs over, the one named last changes fastest.
Arguments:
- queries: bfloat16 [512, 8192], P(('attn', 'grp', 'tp')), may hold values from -100 to 100
- keys: bfloat16 [512, 1024, 256], P(('attn', 'grp', 'tp')), may hold values from -6 to 6
- values: bfloat16 [512, 1024, 256], P(('attn', 'grp', 'tp')), may hold values from -6 to 6
- lengths: int32 [512], P(('attn', 'grp', 'tp')), may hold values from 256 to 1024, as said below
- resid: bfloat16 [512, 7168], P(('attn', 'grp', 'tp')), may hold values from -6 to 6
- assign: int32 [128, 4], P(('attn', 'grp', 'tp')), may hold values from 0 to 3, each once within a row
- matching: int32 [2, 8, 8], P(None, 'attn', 'tp'), may hold values from 0 to 1
- w_out: bfloat16 [8192, 7168], P(None, ('attn', 'tp')), may hold values from -0.5 to 0.5
- gain: float32 [7168], replicated, may hold values from 0.1 to 1.9
- gate_w: bfloat16 [2, 7168, 18432], P('grp', None, ('attn', 'tp')), may hold values from -0.0625 to 0.0625
- up_w: bfloat16 [2, 7168, 18432], P('grp', None, ('attn', 'tp')), may hold values from -0.0625 to 0.0625
- down_w: bfloat16 [2, 18432, 7168], P('grp', ('attn', 'tp')), may hold values from -0.046875 to 0.046875
Outputs:
- layer_out: bfloat16 [512, 7168], P(('attn', 'grp', 'tp'))
Inputs may be any that keep to these rules, and one draw needn't show every extreme that they name: `assign`: each row is an order of the device's 4 requests. `matching`: 1 sends the requests of both devices at one attn, tp position to the other group, so each group serves the requests of exactly half of the devices in each micro-batch. `lengths`: the first request of every device has 1024 live slots.
All inputs are finite; a program needn't handle non-finite values.
Results may differ from a plain program's by a relative error of at most 0.0063.
Values may be sent and summed in bfloat16 or wider, within the bound.
A program may use at most 128 MiB of HBM per device.

v0:
```python
import jax
import jax.numpy as jnp
from jax import lax
from jax.sharding import PartitionSpec as P


def partner_2(value, axis, bit):
    mask = 2**bit
    pairs = [(source, source ^ mask) for source in range(lax.axis_size(axis))]
    return lax.ppermute(value, axis, pairs)


def attend(queries, keys, values, lengths):
    request_count, cache_slots, head_size = keys.shape
    heads = queries.shape[1] // head_size
    query_heads = queries.reshape(request_count, heads, head_size)
    scores = jnp.einsum(
        "rhd,rkd->rhk", query_heads, keys, preferred_element_type=jnp.float32
    ) * head_size ** (-0.5)
    position = lax.broadcasted_iota(jnp.int32, (1, 1, cache_slots), 2)
    visible = position < lengths[:, None, None]
    scores = jnp.where(visible, scores, -1e30)
    highest = jnp.max(scores, axis=-1, keepdims=True)
    expo = jnp.exp(scores - highest)
    weights_bf = (expo / jnp.sum(expo, axis=-1, keepdims=True)).astype(jnp.bfloat16)
    context = jnp.einsum("rhk,rkd->rhd", weights_bf, values, preferred_element_type=jnp.float32)
    return context.astype(jnp.bfloat16).reshape(request_count, heads * head_size)


def to_group(batch_rows, crossing):
    partner = partner_2(batch_rows, "grp", 0)
    return jnp.where(crossing == 1, partner, batch_rows)


def from_group(batch_rows, crossing):
    partner = partner_2(batch_rows, "grp", 0)
    return jnp.where(crossing == 1, partner, batch_rows)


def serve(batch_rows, w_out, gain, gate_w, up_w, down_w):
    context_width, column_count = w_out.shape
    column_start = lax.axis_index(("attn", "tp")) * column_count
    piece = lax.all_gather(batch_rows, ("attn", "tp"), axis=0, tiled=True)
    residual = lax.dynamic_slice_in_dim(piece[:, context_width:], column_start, column_count, 1)
    projected = jnp.dot(piece[:, :context_width], w_out, preferred_element_type=jnp.float32)
    state_columns = (residual.astype(jnp.float32) + projected).astype(jnp.bfloat16)
    state_full = lax.all_gather(state_columns, ("attn", "tp"), axis=1, tiled=True)
    wide = state_full.astype(jnp.float32)
    stat = jnp.mean(wide * wide, axis=-1, keepdims=True)
    normed = (wide * lax.rsqrt(stat + 1e-05) * gain).astype(jnp.bfloat16)
    gate_out = jnp.dot(normed, gate_w[0], preferred_element_type=jnp.float32)
    up_out = jnp.dot(normed, up_w[0], preferred_element_type=jnp.float32)
    act = (jax.nn.silu(gate_out) * up_out).astype(jnp.bfloat16)
    partial_out = jnp.dot(act, down_w[0], preferred_element_type=jnp.float32)
    own_state = state_columns.astype(jnp.float32)
    zero_row = jnp.zeros((), jnp.int32)
    current = lax.dynamic_slice(
        partial_out,
        (zero_row, column_start),
        (batch_rows.shape[0] * lax.axis_size(("attn", "tp")), column_count),
    )
    summed = lax.psum_scatter(
        lax.dynamic_update_slice(partial_out, current + own_state, (zero_row, column_start)),
        ("attn", "tp"),
        scatter_dimension=0,
        tiled=True,
    )
    return summed.astype(jnp.bfloat16)


def per_device(
    queries, keys, values, lengths, resid, assign, matching, w_out, gain, gate_w, up_w, down_w
):
    context = attend(queries, keys, values, lengths)
    bundle = jnp.concatenate([context, resid], axis=1)
    request_count = bundle.shape[0]
    micro_count = matching.shape[0]
    per_batch = request_count // 2
    incoming = []
    for batch_index in range(micro_count):
        picks = assign[0, batch_index * per_batch : (batch_index + 1) * per_batch]
        incoming.append(to_group(bundle[picks], matching[batch_index, 0, 0]))
    served = [serve(batch_rows, w_out, gain, gate_w, up_w, down_w) for batch_rows in incoming]
    returned = [
        from_group(served[batch_index], matching[batch_index, 0, 0])
        for batch_index in range(micro_count)
    ]
    ordered = jnp.concatenate(returned, axis=0)
    inverse = jnp.argsort(assign[0])
    return ordered[inverse]


def solution(mesh):
    placed = (
        P(("attn", "grp", "tp"), None),
        P(("attn", "grp", "tp"), None, None),
        P(("attn", "grp", "tp"), None, None),
        P(("attn", "grp", "tp")),
        P(("attn", "grp", "tp"), None),
        P(("attn", "grp", "tp"), None),
        P(None, "attn", "tp"),
        P(None, ("attn", "tp")),
        P(),
        P("grp", None, ("attn", "tp")),
        P("grp", None, ("attn", "tp")),
        P("grp", ("attn", "tp"), None),
    )
    return jax.shard_map(
        per_device,
        mesh=mesh,
        in_specs=placed,
        out_specs=P(("attn", "grp", "tp"), None),
        check_vma=False,
    )
```

profile of v0, /device:TPU:0, one launch (start us, length us, event | category | flops | bytes accessed | tf_op | source)
XLA Modules:
  0.0 721.9 jit_solution(11405549073469214071)
XLA Ops:
  8.1 1.6 fusion.25
  10.0 2.1 fusion.42
  12.9 2.1 collective-permute-start
  18.6 2.1 collective-permute-start.2
  21.4 1.5 collective-permute-done.2
  23.7 69.4 %all-gather.11.cloned.1.call-done = bf16[64,2,15360]{2,1,0:T(2,128)(2,1)} async-done(((bf16[1,2,15360]{2,1,0:T(2,128)(2,1)}), bf16[64,2,15360]{2,1,0:T(2,128)(2,1)}) %all-gather.11.cloned.1.call-update) | async-done | bytes 3932176 | tf_op jit(solution)/shard_map/all_gather | solution.py:43
  93.1 8.3 %reshape.134 = bf16[128,15360]{1,0:T(8,128)(2,1)} reshape(bf16[64,2,15360]{2,1,0:T(2,128)(2,1)} %all-gather.11.cloned.1.call-done) | data formatting | bytes 7864320
  101.4 1.5 slice-done
  103.1 3.5 fusion.52
  106.7 58.7 %all-gather.13.cloned.1.call-done = bf16[64,2,15360]{2,1,0:T(2,128)(2,1)} async-done(((bf16[1,2,15360]{2,1,0:T(2,128)(2,1)}), bf16[64,2,15360]{2,1,0:T(2,128)(2,1)}) %all-gather.13.cloned.1.call-update) | async-done | bytes 3932176 | tf_op jit(solution)/shard_map/all_gather | solution.py:43
  165.5 8.3 %reshape.136 = bf16[128,15360]{1,0:T(8,128)(2,1)} reshape(bf16[64,2,15360]{2,1,0:T(2,128)(2,1)} %all-gather.13.cloned.1.call-done) | data formatting | bytes 7864320
  173.8 1.5 slice-done.1
  175.5 3.5 fusion.49
  181.3 51.9 %all-gather.7.cloned.1.call-done = bf16[128,7168]{0,1:T(8,128)(2,1)} async-done(((bf16[128,112]{0,1:T(8,128)(2,1)}), bf16[128,7168]{0,1:T(8,128)(2,1)}) %all-gather.7.cloned.1.call-update) | async-done | bytes 1835024 | tf_op jit(solution)/shard_map/all_gather | solution.py:47
  233.2 2.5 fusion.13
  235.7 65.0 %all-gather.9.cloned.1.call-done = bf16[128,7168]{0,1:T(8,128)(2,1)} async-done(((bf16[128,112]{0,1:T(8,128)(2,1)}), bf16[128,7168]{0,1:T(8,128)(2,1)}) %all-gather.9.cloned.1.call-update) | async-done | bytes 1835024 | tf_op jit(solution)/shard_map/all_gather | solution.py:47
  300.7 2.5 fusion.16
  303.2 4.2 fusion.9
  307.7 1.4 fusion.11
  309.1 10.0 %fusion.3 = f32[128,7168]{1,0:T(8,128)} fusion(bf16[1,288,7168]{2,1,0:T(8,128)(2,1)} %param.23, bf16[1,7168,288]{1,2,0:T(8,128)(2,1)} %param.22, bf16[128,7168]{0,1:T(8,128)(2,1)} %all-gather.7.cloned.1.call-done, f32[7168]{0:T(1024)S(1)} %copy-done.2, f32[128]{0:T(128)S(1)} %add_rsqrt_fusion.1, f32[128,288]{0,1:T(8,128)S(1)} %fusion.9), kind=kOutput, calls=%fused_computation.10 | convolution fusion | flops 1060855808 | bytes 13939200 | tf_op jit(solution)/shard_map/dot_general | solution.py:54
  319.1 10.0 %fusion.1 = f32[128,7168]{1,0:T(8,128)} fusion(bf16[1,288,7168]{2,1,0:T(8,128)(2,1)} %param.23, bf16[1,7168,288]{1,2,0:T(8,128)(2,1)} %param.22, bf16[128,7168]{0,1:T(8,128)(2,1)} %all-gather.9.cloned.1.call-done, f32[128]{0:T(128)S(1)} %add_rsqrt_fusion, f32[7168]{0:T(1024)S(1)} %copy-done.2, f32[128,288]{0,1:T(8,128)S(1)} %fusion.11), kind=kOutput, calls=%fused_computation.8 | convolution fusion | flops 1060855808 | bytes 13939200 | tf_op jit(solution)/shard_map/dot_general | solution.py:54
  329.1 1.1 constant_dynamic-slice_fusion
  330.4 1.6 dynamic_update_slice.6
  332.2 1.6 dynamic_update_slice.7
  333.8 371.9 %all-reduce.4 = (bf16[128,7168]{1,0:T(8,128)(2,1)}, bf16[128,7168]{1,0:T(8,128)(2,1)}) all-reduce(f32[128,7168]{1,0:T(8,128)} %dynamic_update_slice.7, f32[128,7168]{1,0:T(8,128)} %dynamic_update_slice.6), channel_id=3, replica_groups=mesh['attn'=8,'grp'=2,'tp'=8] {'attn','tp'}, use_global_device_ids=true, to_apply=%region_5.6.clone | all-reduce | flops 1835008 | bytes 11010048
  705.6 0.9 dynamic-slice_convert_fusion.1
  706.6 1.6 collective-permute-start.1
  708.2 0.9 dynamic-slice_convert_fusion
  710.5 0.9 broadcast_select_fusion.3
  711.5 1.6 collective-permute-done.3
  713.1 0.9 broadcast_select_fusion.2
  714.1 1.2 gather_fusion.2
  (64 shorter events, 10.4 us)
Async XLA Ops:
  6.5 1.6 copy-start
  6.5 5.6 copy-start.7
  6.5 5.7 copy-start.5
  6.5 86.6 %all-gather.11.cloned.1.call-start = ((), (), s32[]{:S(2)}) async-start(), calls=%async_computation.2 | async-start | bytes 3993600 | tf_op jit(solution)/shard_map/all_gather | solution.py:43
  8.1 6.9 copy-start.6
  12.9 4.3 collective-permute-start
  18.0 147.5 %all-gather.13.cloned.1.call-start = ((), (), s32[]{:S(2)}) async-start(), calls=%async_computation.3 | async-start | bytes 3993600 | tf_op jit(solution)/shard_map/all_gather | solution.py:43
  18.6 4.3 collective-permute-start.2
  23.7 209.5 %all-gather.7.cloned.1.call-start = ((), (), s32[]{:S(2)}) async-start(), calls=%async_computation | async-start | bytes 1863680 | tf_op jit(solution)/shard_map/all_gather | solution.py:47
  101.4 1.5 slice-start
  106.7 194.0 %all-gather.9.cloned.1.call-start = ((), (), s32[]{:S(2)}) async-start(), calls=%async_computation.1 | async-start | bytes 1863680 | tf_op jit(solution)/shard_map/all_gather | solution.py:47
  173.8 1.5 slice-start.1
  173.8 5.3 copy-start.9
  175.5 127.7 %copy-start.2 = (f32[7168]{0:T(1024)S(1)}, f32[7168]{0:T(1024)}, u32[]{:S(2)}) copy-start(f32[7168]{0:T(1024)} %param.20) | copy-start | bytes 86020
  303.2 4.3 copy-start.1
  303.2 4.5 copy-start.8
  319.1 11.2 %copy-start.3 = (bf16[128,112]{0,1:T(8,128)(2,1)S(1)}, bf16[128,112]{0,1:T(8,128)(2,1)}, u32[]{:S(2)}) copy-start(bf16[128,112]{0,1:T(8,128)(2,1)} %fusion.52) | copy-start | bytes 86020
  319.1 13.0 %copy-start.4 = (bf16[128,112]{0,1:T(8,128)(2,1)S(1)}, bf16[128,112]{0,1:T(8,128)(2,1)}, u32[]{:S(2)}) copy-start(bf16[128,112]{0,1:T(8,128)(2,1)} %fusion.49) | copy-start | bytes 86020
  706.6 4.0 collective-permute-start.1
  709.1 4.0 collective-permute-start.3
Sparse Core Ops, SparseCore 0:
  18.1 74.9 all-gather.10
  96.2 69.2 all-gather.12
  168.6 64.5 all-gather.6
  236.1 64.5 all-gather.8
where the time goes:
time: 723 us; the launch traced here: 722 us
  blocking collectives  372 us (51%)
  waiting for transfers between devices  250 us (35%)
  matrix products  36.4 us (5%)
  local copies, waits for them, and re-layouts  31.3 us (4%)
  between operations  15.4 us (2%)
  other arithmetic  10.3 us (1%)
    unnamed x1, blocking collectives  372 us
    all_gather x2, waiting for transfers between devices, serve(): piece = lax.all_gather(batch_rows, ('attn', 'tp'), axis=0, tiled=True)  128 us
    all_gather x2, waiting for transfers between devices, serve(): lax.all_gather(state_columns, ('attn', 'tp'), axis=1, tiled=True)  117 us
    dot_general x2, matrix products, serve(): partial_out = jnp.dot(act, down_w[0], preferred_element_type=jnp.float32)  20.1 us
    unnamed x29, local copies, waits for them, and re-layouts  18.7 us
  transfers between devices with their start and end apart: 8, of which 8 were waited for; matrix products, arithmetic and copies ran while one was open for 4% of the time, Pallas kernels for 0%

commit v1 on v0

v1 whole, which is shorter than its diff:
```python
import jax
import jax.numpy as jnp
from jax import lax
from jax.experimental import pallas as pl
from jax.experimental.pallas import tpu as pltpu
from jax.sharding import PartitionSpec as P

D = 7168
CW = 8192
FH = 288
COLS = 112
MESH = pl.DeviceIdType.MESH
F32 = jnp.float32
BF16 = jnp.bfloat16
NT = (((1,), (1,)), ((), ()))


def kernel(
    len_ref, assign_ref, match_ref, q_ref, resid_ref, gain_ref, k_hbm, v_hbm, wo_hbm, g_hbm, u_hbm, d_hbm,
    out_ref,
    kc, vc, wo, wg, wu, wd,
    qs, own_b, got_b, cb, sf, gf, ctx_all, ht, acc_g, acc_u, act_s,
    s1f, s1, s1_got, t1, uf, ub, vb, wf,
    p_send, p_sib, p_own, r2, af, qb, r1, tz, rz, ob, oz,
    kv_sem, w_sem, bs_sem, br_sem, cs_sem, cr_sem, ds_sem, dr_sem, rs_sem, rr_sem,
):
    attn, grp, tp = lax.axis_index("attn"), lax.axis_index("grp"), lax.axis_index("tp")
    x, z, y, c = attn // 2, lax.rem(attn, 2), tp // 2, lax.rem(tp, 2)
    zo, co = 1 - z, 1 - c
    a = x * co + y * c
    b = y * co + x * c

    def dev(x_, z_, y_, c_):
        return (lax.rem(x_, 4) * 2 + z_, grp, lax.rem(y_, 4) * 2 + c_)

    a_right, a_left = dev(x + co, z, y + c, c), dev(x + 3 * co, z, y + 3 * c, c)
    b_right, b_left = dev(x + c, z, y + co, c), dev(x + 3 * c, z, y + 3 * co, c)
    z_peer, sibling = dev(x, zo, y, c), dev(x, z, y, co)
    a1, a2, a3 = lax.rem(a + 1, 4), lax.rem(a + 2, 4), lax.rem(a + 3, 4)
    b1, b2, b3 = lax.rem(b + 1, 4), lax.rem(b + 2, 4), lax.rem(b + 3, 4)

    fetch = []
    for r in range(4):
        for src, dst in ((k_hbm, kc), (v_hbm, vc)):
            fetch.append(pltpu.make_async_copy(src.at[r], dst.at[r], kv_sem.at[len(fetch)]))
            fetch[-1].start()
    loads = [
        pltpu.make_async_copy(src, dst, w_sem.at[i])
        for i, (src, dst) in enumerate(((wo_hbm, wo), (g_hbm, wg), (u_hbm, wu), (d_hbm, wd)))
    ]
    for load in loads:
        load.start()

    barrier = pltpu.get_barrier_semaphore()
    partner = (attn, 1 - grp, tp)
    others = [partner]
    for k in range(1, 8):
        others.append((lax.rem(attn + k, 8), grp, tp))
        others.append((attn, grp, lax.rem(tp + k, 8)))
    for other in others:
        pl.semaphore_signal(barrier, inc=1, device_id=other, device_id_type=MESH)

    wide_q = q_ref[...].astype(F32)
    for h in range(32):
        for half in range(2):
            first = h * 256 + half * 128
            qs[half, pl.ds(h, 4, stride=32), :] = wide_q[:, first : first + 128]
    contexts = []
    slot = lax.broadcasted_iota(jnp.int32, (32, 1024), 1)
    for r in range(4):
        fetch[2 * r].wait()
        scores = lax.dot_general(
            jnp.concatenate([qs[half, r * 32 : (r + 1) * 32] for half in range(2)], axis=1).astype(BF16),
            kc[r],
            NT,
            preferred_element_type=F32,
        ) * (256 ** -0.5)
        scores = jnp.where(slot < len_ref[r], scores, -1e30)
        expo = jnp.exp(scores - jnp.max(scores, axis=-1, keepdims=True))
        probs = (expo / jnp.sum(expo, axis=-1, keepdims=True)).astype(BF16)
        fetch[2 * r + 1].wait()
        contexts.append(jnp.dot(probs, vc[r], preferred_element_type=F32))
    for p in range(4):
        chosen = contexts[0]
        for r in range(1, 4):
            chosen = jnp.where(assign_ref[p] == r, contexts[r], chosen)
        own_b[p * 32 : (p + 1) * 32] = chosen.astype(BF16)
    pl.semaphore_wait(barrier, 15)

    started = []

    def push(src, dst, s_sem, r_sem, i, to):
        copy = pltpu.make_async_remote_copy(
            src_ref=src, dst_ref=dst, send_sem=s_sem.at[i], recv_sem=r_sem.at[i],
            device_id=to, device_id_type=MESH,
        )
        copy.start()
        started.append(copy)

    def landed(dst, s_sem, r_sem, i):
        pltpu.make_async_remote_copy(
            src_ref=dst, dst_ref=dst, send_sem=s_sem.at[i], recv_sem=r_sem.at[i],
            device_id=sibling, device_id_type=MESH,
        ).wait_recv()

    def gather(block, slab, s_sem, r_sem, ready):
        def send(ref, i, to):
            push(ref, ref, s_sem, r_sem, i, to)

        def wait(ref, i):
            landed(ref, s_sem, r_sem, i)

        own = block(z, a)
        send(own, 1, a_right)
        send(own, 2, a_left)
        send(own, 0, z_peer)
        wait(block(zo, a), 0)
        send(block(zo, a), 3, a_right)
        send(block(zo, a), 4, a_left)
        wait(block(z, a3), 1)
        send(block(z, a3), 5, a_right)
        wait(block(z, a1), 2)
        wait(block(zo, a1), 4)
        send(block(zo, a1), 6, a_left)
        wait(block(zo, a3), 3)
        wait(block(z, a2), 5)
        ready(z)
        send(slab(z, b), 7, b_right)
        send(slab(z, b), 8, b_left)
        wait(block(zo, a2), 6)
        ready(zo)
        send(slab(zo, b), 9, b_right)
        send(slab(zo, b), 10, b_left)
        send(slab(z, b), 13, sibling)
        send(slab(zo, b), 14, sibling)
        yield
        wait(slab(z, b3), 7)
        send(slab(z, b3), 11, b_right)
        send(slab(z, b3), 15, sibling)
        wait(slab(z, b1), 8)
        send(slab(z, b1), 16, sibling)
        wait(slab(zo, b1), 10)
        send(slab(zo, b1), 12, b_left)
        send(slab(zo, b1), 17, sibling)
        wait(slab(zo, b3), 9)
        send(slab(zo, b3), 18, sibling)
        wait(slab(z, b2), 11)
        send(slab(z, b2), 19, sibling)
        wait(slab(zo, b2), 12)
        send(slab(zo, b2), 20, sibling)
        yield

    def from_sibling(slab, s_sem, r_sem):
        a_s1, a_s2, a_s3 = a1, a2, a3
        for i, (zv, bv) in enumerate(
            ((z, a), (zo, a), (z, a_s3), (z, a_s1), (zo, a_s1), (zo, a_s3), (z, a_s2), (zo, a_s2))
        ):
            landed(slab(zv, bv), s_sem, r_sem, 13 + i)

    push(own_b, got_b, rs_sem, rr_sem, 0, partner)

    wide_r = resid_ref[...].astype(F32)
    ordered = []
    for p in range(4):
        chosen = wide_r[0:1]
        for r in range(1, 4):
            chosen = jnp.where(assign_ref[p] == r, wide_r[r : r + 1], chosen)
        ordered.append(chosen)
    ordered = jnp.concatenate(ordered, axis=0)
    s1f[...] = jnp.zeros_like(s1f)
    for n in range(8):
        for t in range(8):
            first = n * 896 + t * COLS
            s1f[n, (t % 4) * 4 : (t % 4) * 4 + 4, (t // 4) * 128 : (t // 4) * 128 + COLS] = ordered[
                :, first : first + COLS
            ]
    s1[...] = s1f[...].astype(BF16)
    push(s1, s1_got, rs_sem, rr_sem, 1, partner)

    swap0, swap1 = match_ref[0], match_ref[1]
    row = lax.broadcasted_iota(jnp.int32, (128, 256), 0)
    landed(got_b, rs_sem, rr_sem, 0)
    cb[z, a] = jnp.where(jnp.where(row < 64, swap0, swap1) == 1, got_b[...], own_b[...])

    def ctx_slab(plane):
        return lambda zv, bv: ctx_all.at[(plane * 2 + zv) * 4 + bv]

    def ctx_ready(zv):
        for half in range(2):
            sf[half] = cb[zv, :, :, half * 128 : (half + 1) * 128].astype(F32).reshape(512, 128)
        for h in range(32):
            for half in range(2):
                first = h * 256 + half * 128
                ctx_all[(c * 2 + zv) * 4 + b, :, first : first + 128] = sf[
                    half, pl.ds(h, 16, stride=32), :
                ].astype(BF16)

    steps = gather(lambda zv, av: cb.at[zv, av], ctx_slab(c), bs_sem, br_sem, ctx_ready)
    next(steps)

    landed(s1_got, rs_sem, rr_sem, 1)
    row = lax.rem(lax.broadcasted_iota(jnp.int32, (8, 16, 256), 1), 4)
    served = jnp.where(jnp.where(row < 2, swap0, swap1) == 1, s1_got[...], s1[...])
    s1_got[...] = served
    t1[attn] = s1_got[attn]
    for k in range(1, 8):
        to = lax.rem(attn + k, 8)
        push(s1_got.at[to], t1.at[attn], rs_sem, rr_sem, 1 + k, (to, grp, tp))
    loads[1].wait()
    loads[2].wait()

    def scale(i, _):
        cols = pl.ds(pl.multiple_of(i * 512, 512), 512)
        by = gain_ref[:, cols]
        wg[:, cols] = (wg[:, cols].astype(F32) * by).astype(BF16)
        wu[:, cols] = (wu[:, cols].astype(F32) * by).astype(BF16)
        return 0

    lax.fori_loop(0, 7, scale, 0)
    for k in range(1, 8):
        landed(t1.at[lax.rem(attn + 8 - k, 8)], rs_sem, rr_sem, 1 + k)
    for n in range(8):
        part = t1[n].astype(F32)
        for t in range(8):
            uf[t, n * 4 : n * 4 + 4, :] = part[
                (t % 4) * 4 : (t % 4) * 4 + 4, (t // 4) * 128 : (t // 4) * 128 + 128
            ]
    ub[...] = uf[...].astype(BF16)
    vb[tp] = ub[tp]
    for k in range(1, 8):
        to = lax.rem(tp + k, 8)
        push(ub.at[to], vb.at[tp], rs_sem, rr_sem, 8 + k, (attn, grp, to))
    lax.fori_loop(7, 14, scale, 0)
    next(steps)
    for k in range(1, 8):
        landed(vb.at[lax.rem(tp + 8 - k, 8)], rs_sem, rr_sem, 8 + k)
    for t in range(8):
        part = vb[t].astype(F32)
        for n in range(8):
            place = ((t % 2 * 2 + n % 2) * 4 + (n // 2 if t % 2 else t // 2)) * 4
            place = (place + (t // 2 if t % 2 else n // 2)) * 4
            wf[place : place + 4, :] = part[n * 4 : n * 4 + 4]
    resid_t = wf[...].T[:COLS]
    from_sibling(ctx_slab(co), bs_sem, br_sem)
    loads[0].wait()

    def project(i, acc):
        cols = pl.ds(pl.multiple_of(i * 1024, 1024), 1024)
        rows = ctx_all[:, :, cols].reshape(256, 1024)
        return acc + lax.dot_general(wo[:, cols], rows, NT, preferred_element_type=F32)

    proj = lax.fori_loop(0, CW // 1024, project, jnp.zeros((COLS, 256), F32))
    me = ((c * 2 + z) * 4 + b) * 4 + a
    ht[me] = (resid_t + proj).astype(BF16)

    def ht_slab(plane):
        return lambda zv, bv: ht.at[pl.ds(((plane * 2 + zv) * 4 + bv) * 4, 4)]

    steps = gather(
        lambda zv, av: ht.at[((c * 2 + zv) * 4 + b) * 4 + av], ht_slab(c), cs_sem, cr_sem, lambda zv: None
    )
    next(steps)
    next(steps)
    from_sibling(ht_slab(co), cs_sem, cr_sem)

    acc_g[...] = jnp.zeros_like(acc_g)
    acc_u[...] = jnp.zeros_like(acc_u)

    def features(xv, zv):
        parts = []
        for yv in range(4):
            parts.append(ht[(zv * 4 + yv) * 4 + xv])
            parts.append(ht[((2 + zv) * 4 + xv) * 4 + yv])
        return jnp.concatenate(parts, axis=0)

    def expand(i, squares):
        cols = pl.ds(pl.multiple_of(i * 896, 128), 896)
        part = features(i // 2, lax.rem(i, 2))
        acc_g[...] += jnp.dot(wg[:, cols], part, preferred_element_type=F32)
        acc_u[...] += jnp.dot(wu[:, cols], part, preferred_element_type=F32)
        wide = part.astype(F32)
        return squares + jnp.sum((wide * wide).reshape(112, 8, 256), axis=0)

    squares = lax.fori_loop(0, 8, expand, jnp.zeros((8, 256), F32))
    factor = lax.rsqrt(jnp.sum(squares, axis=0, keepdims=True) * (1.0 / D) + 1e-5)
    gate = acc_g[...] * factor
    act = gate / (1.0 + jnp.exp(-gate)) * (acc_u[...] * factor)
    act_s[...] = act.T.astype(BF16)

    loads[3].wait()
    width = 1024
    act_other = act_s[pl.ds(pl.multiple_of(co * 128, 128), 128), :]
    for j in range(D // width):
        cols = pl.ds(j * width, width)
        part = jnp.dot(act_other, wd[:, cols], preferred_element_type=F32)
        p_send[:, :, cols] = part.astype(BF16).reshape(8, 16, width)
        push(p_send.at[:, :, cols], p_sib.at[:, :, cols], ds_sem, dr_sem, j, sibling)
    act_mine = act_s[pl.ds(pl.multiple_of(c * 128, 128), 128), :]
    for j in range(D // width):
        cols = pl.ds(j * width, width)
        part = jnp.dot(act_mine, wd[:, cols], preferred_element_type=F32)
        landed(p_sib.at[:, :, cols], ds_sem, dr_sem, j)
        total = part + p_sib[:, :, cols].reshape(128, width).astype(F32)
        p_own[:, :, cols] = total.astype(BF16).reshape(8, 16, width)

    def reduce_ring(part, spots, left, right, kl, kr, ko, first):
        def send(ref, i, to):
            push(ref, spots.at[i], ds_sem, dr_sem, first + i, to)

        def wait(i):
            landed(spots.at[i], ds_sem, dr_sem, first + i)

        send(part(0, ko), 0, left)
        send(part(1, ko), 1, right)
        send(part(1, kl), 3, left)
        send(part(0, kr), 4, right)
        yield
        for i, p, k, to, j in ((0, 0, kl, left, 2), (1, 1, kr, right, 5)):
            wait(i)
            ref = part(p, k)
            ref[...] = (ref[...].astype(F32) + spots[i].astype(F32)).astype(BF16)
            send(ref, j, to)
        for i in (3, 4, 2, 5):
            wait(i)
        yield

    zs = (z, zo)
    steps = reduce_ring(lambda p, k: p_own.at[zs[p] * 4 + k], r2, b_left, b_right, b3, b1, b2, 7)
    next(steps)

    lane = lax.broadcasted_iota(jnp.int32, (16, 256), 1)
    sub = lax.broadcasted_iota(jnp.int32, (16, 256), 0)
    hidden = jnp.zeros((16, 1792), F32)
    for q in range(4):
        pick = jnp.where(lane == me * 4 + sub - q * 4, 1.0, 0.0)
        pick = jnp.where((sub >= q * 4) & (sub < q * 4 + 4), pick, 0.0).astype(BF16)
        rows = jnp.concatenate([features(q, 0), features(q, 1)], axis=0)
        hidden = hidden + lax.dot_general(pick, rows, NT, preferred_element_type=F32)
    next(steps)
    for p in range(2):
        af[...] = (
            p_own[zs[p] * 4 + b].astype(F32) + r2[2 + p].astype(F32) + r2[4 + p].astype(F32)
        )
        for av in range(4):
            for q in range(4):
                gf[q * 4 : q * 4 + 4, av * 2048 : av * 2048 + 1792] = af[
                    av * 4 : av * 4 + 4, q * 1792 : (q + 1) * 1792
                ]
        for av in range(4):
            qb[p, av] = gf[:, av * 2048 : av * 2048 + 1792].astype(BF16)
    steps = reduce_ring(lambda p, k: qb.at[p, k], r1, a_left, a_right, a3, a1, a2, 13)
    next(steps)
    next(steps)
    tz[...] = (qb[1, a].astype(F32) + r1[3].astype(F32) + r1[5].astype(F32)).astype(BF16)
    push(tz, rz, ds_sem, dr_sem, 19, z_peer)
    mine = qb[0, a].astype(F32) + r1[2].astype(F32) + r1[4].astype(F32)
    landed(rz, ds_sem, dr_sem, 19)
    ob[...] = (hidden + (mine + rz[...].astype(F32))).astype(BF16)

    push(ob, oz, rs_sem, rr_sem, 16, partner)
    landed(oz, rs_sem, rr_sem, 16)
    row = lax.rem(lax.broadcasted_iota(jnp.int32, (16, 1792), 0), 4)
    swapped = jnp.where(row < 2, swap0, swap1) == 1
    final = jnp.where(swapped, oz[...].astype(F32), ob[...].astype(F32))
    request = lax.broadcasted_iota(jnp.int32, (4, 1792), 0)
    for q in range(4):
        rows = jnp.zeros((4, 1792), F32)
        for p in range(4):
            one = jnp.broadcast_to(final[q * 4 + p : q * 4 + p + 1], (4, 1792))
            rows = jnp.where(request == assign_ref[p], one, rows)
        out_ref[:, q * 1792 : (q + 1) * 1792] = rows.astype(BF16)
    for copy in started:
        copy.wait_send()


def per_device(
    queries, keys, values, lengths, resid, assign, matching, w_out, gain, gate_w, up_w, down_w
):
    smem = pl.BlockSpec(memory_space=pltpu.SMEM)
    vmem = pl.BlockSpec(memory_space=pltpu.VMEM)
    hbm = pl.BlockSpec(memory_space=pl.ANY)
    dma = pltpu.SemaphoreType.DMA
    scratch = (
        ((4, 1024, 256), BF16),
        ((4, 1024, 256), BF16),
        ((COLS, CW), BF16),
        ((FH, D), BF16),
        ((FH, D), BF16),
        ((FH, D), BF16),
        ((2, 128, 128), F32),
        ((128, 256), BF16),
        ((128, 256), BF16),
        ((2, 4, 128, 256), BF16),
        ((2, 512, 128), F32),
        ((16, CW), F32),
        ((16, 16, CW), BF16),
        ((64, COLS, 256), BF16),
        ((FH, 256), F32),
        ((FH, 256), F32),
        ((256, FH), BF16),
        ((8, 16, 256), F32),
        ((8, 16, 256), BF16),
        ((8, 16, 256), BF16),
        ((8, 16, 256), BF16),
        ((8, 32, 128), F32),
        ((8, 32, 128), BF16),
        ((8, 32, 128), BF16),
        ((256, 128), F32),
        ((8, 16, D), BF16),
        ((8, 16, D), BF16),
        ((8, 16, D), BF16),
        ((6, 16, D), BF16),
        ((16, D), F32),
        ((2, 4, 16, 1792), BF16),
        ((6, 16, 1792), BF16),
        ((16, 1792), BF16),
        ((16, 1792), BF16),
        ((16, 1792), BF16),
        ((16, 1792), BF16),
    )
    return pl.pallas_call(
        kernel,
        out_shape=jax.ShapeDtypeStruct((4, D), BF16),
        in_specs=[smem] * 3 + [vmem] * 3 + [hbm] * 6,
        out_specs=vmem,
        scratch_shapes=[pltpu.VMEM(shape, dtype) for shape, dtype in scratch]
        + [dma((n,)) for n in (8, 4, 21, 21, 21, 21, 20, 20, 17, 17)],
        compiler_params=pltpu.CompilerParams(
            collective_id=0, has_side_effects=True, vmem_limit_bytes=60 * 1024 * 1024
        ),
    )(
        lengths, assign[0], matching[:, 0, 0], queries, resid, gain[None],
        keys, values, w_out.T, gate_w[0].T, up_w[0].T, down_w[0],
    )


def solution(mesh):
    rows = P(("attn", "grp", "tp"), None)
    cache = P(("attn", "grp", "tp"), None, None)
    placed = (
        rows,
        cache,
        cache,
        P(("attn", "grp", "tp")),
        rows,
        rows,
        P(None, "attn", "tp"),
        P(None, ("attn", "tp")),
        P(),
        P("grp", None, ("attn", "tp")),
        P("grp", None, ("attn", "tp")),
        P("grp", ("attn", "tp"), None),
    )
    return jax.shard_map(
        per_device, mesh=mesh, in_specs=placed, out_specs=rows, check_vma=False
    )
```

time: 723 us -> 102 us (0.14)
  blocking collectives: 372 us -> 0 us
  waiting for transfers between devices: 250 us -> 0 us
  Pallas kernels: 0 us -> 99.1 us
  matrix products: 36.4 us -> 0 us
  local copies, waits for them, and re-layouts: 31.3 us -> 1.46 us
  between operations: 15.4 us -> 0.01 us
  other arithmetic: 10.3 us -> 0 us
    unnamed x1 -> x0, blocking collectives: 372 us -> none
    all_gather x4 -> x0, waiting for transfers between devices: 245 us -> none  [the longest x2 128 us: serve(): piece = lax.all_gather(batch_rows, ('attn', 'tp'), axis=0, tiled=True)]
    pallas_call x0 -> x1, Pallas kernels: none -> 99.1 us  [per_device(): pl.pallas_call(kernel, out_shape=jax.ShapeDtypeStruct((4, D), BF16), in_s...]
    dot_general x8 -> x0, matrix products: 36.4 us -> none  [the longest x2 20.1 us: serve(): partial_out = jnp.dot(act, down_w[0], preferred_element_type=jnp.float32)]
    unnamed x29 -> x1, local copies, waits for them, and re-layouts: 18.7 us -> 1.46 us
  transfers between devices with their start and end apart: 8 -> 0, of which waited for: 8 -> 0; matrix products, arithmetic and copies ran while one was open for 4% -> 0% of each run, Pallas kernels for 0% -> 0%
where the time goes in v1:
time: 102 us; the launch traced here: 101 us
  Pallas kernels  99.1 us (97%)
  local copies, waits for them, and re-layouts  1.46 us (1%)
    pallas_call x1, Pallas kernels, per_device(): pl.pallas_call(kernel, out_shape=jax.ShapeDtypeStruct((4, D), BF16), in_s...  99.1 us

profile of v1, /device:TPU:0, one launch (start us, length us, event | category | flops | bytes accessed | tf_op | source)
XLA Modules:
  0.0 100.6 jit_solution(335420380846787116)
XLA Ops:
  0.0 99.1 %shard_map.118 = bf16[4,7168]{1,0:T(4,128)(2,1)} custom-call(s32[4]{0:T(128)} %len_ref.1, s32[4]{0:T(128)} %bitcast.16, s32[2]{0:T(128)} %bitcast.17, bf16[4,8192]{1,0:T(4,128)(2,1)} %q_ref.1, bf16[4,7168]{1,0:T(4,128)(2,1)} %resid_ref.1, f32[1,7168]{1,0:T(1,128)} %bitcast.15, bf16[4,1024,256]{2,1,0:T(8,128)(2,1)} %k_hbm.1, bf16[4,1024,256]{2,1,0:T(8,128)(2,1)} %v_hbm.1, ...), custom_call_target="tpu_custom_call" | custom-call | tf_op jit(solution)/shard_map/pallas_call | solution.py:421
  99.1 1.5 %copy.14 = bf16[4,7168]{1,0:T(4,128)(2,1)} copy(bf16[4,7168]{1,0:T(4,128)(2,1)} %shard_map.118) | data formatting | bytes 114688

commit v2 on v0

v2 whole, which is shorter than its diff:
```python
import jax
import jax.numpy as jnp
from jax import lax
from jax.experimental import pallas as pl
from jax.experimental.pallas import tpu as pltpu
from jax.sharding import PartitionSpec as P

D = 7168
CW = 8192
FH = 288
COLS = 112
MESH = pl.DeviceIdType.MESH
F32 = jnp.float32
BF16 = jnp.bfloat16
NT = (((1,), (1,)), ((), ()))


def kernel(
    len_ref, assign_ref, match_ref, q_ref, resid_hbm, gain_hbm, k_hbm, v_hbm, wo_hbm, g_hbm, u_hbm, d_hbm,
    out_ref,
    kc, vc, wo, wg, wu, wd, resid_ref, gain_ref,
    qs, own_b, got_b, cb, sf, ctx_all, ht, acc_g, acc_u, act_s,
    s1f, s1, s1_got, t1, uf, ub, vb, wf, wt,
    pf, p_send, p_sib, p_own, r2, qf, qb, r1, t0, tp0, tz, got_peer, got_partner, got_cross, hid, hid_got,
    kv_sem, w_sem, bs_sem, br_sem, cs_sem, cr_sem, ds_sem, dr_sem, rs_sem, rr_sem,
):
    attn, grp, tp = lax.axis_index("attn"), lax.axis_index("grp"), lax.axis_index("tp")
    x, z, y, c = attn // 2, lax.rem(attn, 2), tp // 2, lax.rem(tp, 2)
    zo, co = 1 - z, 1 - c
    zs = (z, zo)
    a = x * co + y * c
    b = y * co + x * c

    def dev(x_, z_, y_, c_):
        return (lax.rem(x_, 4) * 2 + z_, grp, lax.rem(y_, 4) * 2 + c_)

    a_other = [dev(x + k * co, z, y + k * c, c) for k in range(4)]
    b_right, b_left = dev(x + c, z, y + co, c), dev(x + 3 * c, z, y + 3 * co, c)
    z_peer, sibling = dev(x, zo, y, c), dev(x, z, y, co)
    partner = (attn, 1 - grp, tp)
    cross = (x * 2 + zo, 1 - grp, tp)
    ak = [lax.rem(a + k, 4) for k in range(4)]
    b1, b2, b3 = lax.rem(b + 1, 4), lax.rem(b + 2, 4), lax.rem(b + 3, 4)

    fetch = []
    for r in range(4):
        for src, dst in ((k_hbm, kc), (v_hbm, vc)):
            fetch.append(pltpu.make_async_copy(src.at[r], dst.at[r], kv_sem.at[len(fetch)]))
            fetch[-1].start()
    loads = [
        pltpu.make_async_copy(src, dst, w_sem.at[i])
        for i, (src, dst) in enumerate(
            ((resid_hbm, resid_ref), (gain_hbm, gain_ref), (g_hbm, wg), (u_hbm, wu), (wo_hbm, wo), (d_hbm, wd))
        )
    ]
    for load in loads:
        load.start()

    barrier = pltpu.get_barrier_semaphore()
    others = [partner, cross]
    for k in range(1, 8):
        others.append((lax.rem(attn + k, 8), grp, tp))
        others.append((attn, grp, lax.rem(tp + k, 8)))
    for other in others:
        pl.semaphore_signal(barrier, inc=1, device_id=other, device_id_type=MESH)

    started = []

    def push(src, dst, s_sem, r_sem, i, to):
        copy = pltpu.make_async_remote_copy(
            src_ref=src, dst_ref=dst, send_sem=s_sem.at[i], recv_sem=r_sem.at[i],
            device_id=to, device_id_type=MESH,
        )
        copy.start()
        started.append(copy)

    def landed(dst, s_sem, r_sem, i):
        pltpu.make_async_remote_copy(
            src_ref=dst, dst_ref=dst, send_sem=s_sem.at[i], recv_sem=r_sem.at[i],
            device_id=sibling, device_id_type=MESH,
        ).wait_recv()

    wide_q = q_ref[...].astype(F32)
    for h in range(32):
        for half in range(2):
            first = h * 256 + half * 128
            qs[half, pl.ds(h, 4, stride=32), :] = wide_q[:, first : first + 128]
    slot = lax.broadcasted_iota(jnp.int32, (32, 1024), 1)
    swaps = (match_ref[0], match_ref[1])

    def attend(r):
        fetch[2 * r].wait()
        query = jnp.concatenate([qs[half, r * 32 : (r + 1) * 32] for half in range(2)], axis=1).astype(BF16)
        scores = lax.dot_general(query, kc[r], NT, preferred_element_type=F32) * (256 ** -0.5)
        scores = jnp.where(slot < len_ref[r], scores, -1e30)
        expo = jnp.exp(scores - jnp.max(scores, axis=-1, keepdims=True))
        probs = (expo / jnp.sum(expo, axis=-1, keepdims=True)).astype(BF16)
        fetch[2 * r + 1].wait()
        return jnp.dot(probs, vc[r], preferred_element_type=F32)

    contexts = [attend(r) for r in range(4)]
    for p in range(4):
        chosen = contexts[0]
        for r in range(1, 4):
            chosen = jnp.where(assign_ref[p] == r, contexts[r], chosen)
        own_b[p * 32 : p * 32 + 32] = chosen.astype(BF16)
    pl.semaphore_wait(barrier, 16)

    def gather(block, part, other, s_sem, r_sem, ready):
        def send(ref, i, to):
            push(ref, ref, s_sem, r_sem, i, to)

        def wait(ref, i):
            landed(ref, s_sem, r_sem, i)

        def ring_1(p):
            for k in (1, 3, 2):
                send(block(p, a), 3 * p + k, a_other[k])

        def ring_2(p):
            for k in (1, 3, 2):
                wait(block(p, ak[4 - k]), 3 * p + k)
            ready(p)
            first, second = ((7, b_right), (8, b_left)) if p == 0 else ((10, b_left), (9, b_right))
            send(part(p, b), *first)
            send(part(p, b), *second)
            send(part(p, b), 13 + p, sibling)

        ring_1(0)
        send(block(0, a), 0, z_peer)
        yield
        ring_2(0)
        wait(block(1, a), 0)
        ring_1(1)
        yield
        ring_2(1)
        yield
        wait(part(0, b3), 7)
        send(part(0, b3), 11, b_right)
        send(part(0, b3), 15, sibling)
        wait(part(0, b1), 8)
        send(part(0, b1), 16, sibling)
        yield
        wait(part(1, b1), 10)
        send(part(1, b1), 12, b_left)
        send(part(1, b1), 17, sibling)
        wait(part(1, b3), 9)
        send(part(1, b3), 18, sibling)
        yield
        wait(part(0, b2), 11)
        send(part(0, b2), 19, sibling)
        wait(part(1, b2), 12)
        send(part(1, b2), 20, sibling)
        yield
        for i, (zv, k) in enumerate(
            ((z, 0), (zo, 0), (z, 3), (z, 1), (zo, 1), (zo, 3), (z, 2), (zo, 2))
        ):
            wait(other(zv, ak[k]), 13 + i)
        yield

    me = ((c * 2 + z) * 4 + b) * 4 + a

    def residual():
        loads[0].wait()
        wide_r = resid_ref[...].astype(F32)
        ordered = []
        for p in range(4):
            chosen = wide_r[0:1]
            for r in range(1, 4):
                chosen = jnp.where(assign_ref[p] == r, wide_r[r : r + 1], chosen)
            ordered.append(chosen)
        ordered = jnp.concatenate(ordered, axis=0)
        s1f[...] = jnp.zeros_like(s1f)
        for n in range(8):
            for t in range(8):
                first = n * 896 + t * COLS
                s1f[n, (t % 4) * 4 : (t % 4) * 4 + 4, (t // 4) * 128 : (t // 4) * 128 + COLS] = ordered[
                    :, first : first + COLS
                ]
        s1[...] = s1f[...].astype(BF16)
        push(s1, s1_got, rs_sem, rr_sem, 1, partner)
        yield
        landed(s1_got, rs_sem, rr_sem, 1)
        row = lax.rem(lax.broadcasted_iota(jnp.int32, (8, 16, 256), 1), 4)
        served = jnp.where(jnp.where(row < 2, swaps[0], swaps[1]) == 1, s1_got[...], s1[...])
        s1_got[...] = served
        t1[attn] = s1_got[attn]
        for k in range(1, 8):
            to = lax.rem(attn + k, 8)
            push(s1_got.at[to], t1.at[attn], rs_sem, rr_sem, 1 + k, (to, grp, tp))
        yield
        for k in range(1, 8):
            landed(t1.at[lax.rem(attn + 8 - k, 8)], rs_sem, rr_sem, 1 + k)
        for n in range(8):
            part = t1[n].astype(F32)
            for t in range(8):
                uf[t, n * 4 : n * 4 + 4, :] = part[
                    (t % 4) * 4 : (t % 4) * 4 + 4, (t // 4) * 128 : (t // 4) * 128 + 128
                ]
        ub[...] = uf[...].astype(BF16)
        vb[tp] = ub[tp]
        for k in range(1, 8):
            to = lax.rem(tp + k, 8)
            push(ub.at[to], vb.at[tp], rs_sem, rr_sem, 8 + k, (attn, grp, to))
        yield
        for k in range(1, 8):
            landed(vb.at[lax.rem(tp + 8 - k, 8)], rs_sem, rr_sem, 8 + k)
        for t in range(8):
            part = vb[t].astype(F32)
            for n in range(8):
                plane, zv = t % 2, n % 2
                bv, av = (n // 2, t // 2) if plane else (t // 2, n // 2)
                place = (((plane * 2 + zv) * 4 + bv) * 4 + av) * 4
                wf[place : place + 4, :] = part[n * 4 : n * 4 + 4]
        wt[...] = wf[...].T
        yield

    def scaling():
        for i in (1, 2, 3):
            loads[i].wait()

        def scale(i, _):
            cols = pl.ds(pl.multiple_of(i * 512, 512), 512)
            by = gain_ref[:, cols]
            wg[:, cols] = (wg[:, cols].astype(F32) * by).astype(BF16)
            wu[:, cols] = (wu[:, cols].astype(F32) * by).astype(BF16)
            return 0

        for first, last in ((0, 5), (5, 10), (10, 14)):
            lax.fori_loop(first, last, scale, 0)
            yield

    push(own_b, got_b, rs_sem, rr_sem, 0, partner)
    residual_steps, scaling_steps = residual(), scaling()
    next(residual_steps)
    row = lax.broadcasted_iota(jnp.int32, (128, 256), 0)
    landed(got_b, rs_sem, rr_sem, 0)
    cb[z, a] = jnp.where(jnp.where(row < 64, swaps[0], swaps[1]) == 1, got_b[...], own_b[...])

    def ready(p):
        for half in range(2):
            sf[half] = cb[zs[p], :, :, half * 128 : (half + 1) * 128].astype(F32).reshape(512, 128)
        for h in range(32):
            for half in range(2):
                first = h * 256 + half * 128
                ctx_all[(c * 2 + zs[p]) * 4 + b, :, first : first + 128] = sf[
                    half, pl.ds(h, 16, stride=32), :
                ].astype(BF16)

    steps = gather(
        lambda p, av: cb.at[zs[p], av],
        lambda p, bv: ctx_all.at[(c * 2 + zs[p]) * 4 + bv],
        lambda zv, bv: ctx_all.at[(co * 2 + zv) * 4 + bv],
        bs_sem,
        br_sem,
        ready,
    )
    next(steps)
    next(residual_steps)
    next(steps)
    next(scaling_steps)
    next(steps)
    next(residual_steps)
    next(scaling_steps)
    next(steps)
    next(scaling_steps)
    next(steps)
    next(residual_steps)
    next(steps)
    loads[4].wait()

    def project(plane):
        def step(i, acc):
            cols = pl.ds(pl.multiple_of(i * 1024, 1024), 1024)
            rows = ctx_all[pl.ds(plane * 8, 8), :, cols].reshape(128, 1024)
            return acc + lax.dot_general(wo[:, cols], rows, NT, preferred_element_type=F32)

        total = lax.fori_loop(0, CW // 1024, step, jnp.zeros((COLS, 128), F32))
        lanes = pl.ds(pl.multiple_of(plane * 128, 128), 128)
        ht[me, :, lanes] = (wt[:COLS, lanes] + total).astype(BF16)

    project(c)
    next(steps)
    project(co)

    steps = gather(
        lambda p, av: ht.at[((c * 2 + zs[p]) * 4 + b) * 4 + av],
        lambda p, bv: ht.at[pl.ds(((c * 2 + zs[p]) * 4 + bv) * 4, 4)],
        lambda zv, bv: ht.at[pl.ds(((co * 2 + zv) * 4 + bv) * 4, 4)],
        cs_sem,
        cr_sem,
        lambda p: None,
    )
    for _ in range(7):
        next(steps)

    def features(xv, zv):
        parts = []
        for yv in range(4):
            parts.append(ht[(zv * 4 + yv) * 4 + xv])
            parts.append(ht[((2 + zv) * 4 + xv) * 4 + yv])
        return jnp.concatenate(parts, axis=0)

    acc_g[...] = jnp.zeros_like(acc_g)
    acc_u[...] = jnp.zeros_like(acc_u)

    def expand(i, squares):
        cols = pl.ds(pl.multiple_of(i * 896, 128), 896)
        part = features(i // 2, lax.rem(i, 2))
        acc_g[...] += jnp.dot(wg[:, cols], part, preferred_element_type=F32)
        acc_u[...] += jnp.dot(wu[:, cols], part, preferred_element_type=F32)
        wide = part.astype(F32)
        return squares + jnp.sum((wide * wide).reshape(112, 8, 256), axis=0)

    squares = lax.fori_loop(0, 8, expand, jnp.zeros((8, 256), F32))
    factor = lax.rsqrt(jnp.sum(squares, axis=0, keepdims=True) * (1.0 / D) + 1e-5)
    gate = acc_g[...] * factor
    act = gate / (1.0 + jnp.exp(-gate)) * (acc_u[...] * factor)
    act_s[...] = act.T.astype(BF16)

    loads[5].wait()
    lhs = jnp.concatenate(
        [act_s[pl.ds(pl.multiple_of(k * 128, 128), 128), :] for k in (co, c)], axis=0
    )

    def reduction(h):
        for j in range(2):
            cols = pl.ds(j * 1792, 1792)
            part = jnp.dot(lhs, wd[:, pl.ds(h * 3584 + j * 1792, 1792)], preferred_element_type=F32)
            p_send[h, :, :, cols] = part[:128].astype(BF16).reshape(8, 16, 1792)
            pf[h, :, :, cols] = part[128:].reshape(8, 16, 1792)
        push(p_send.at[h], p_sib.at[h], ds_sem, dr_sem, h, sibling)
        yield
        landed(p_sib.at[h], ds_sem, dr_sem, h)
        p_own[h] = (pf[h] + p_sib[h].astype(F32)).astype(BF16)

        def slab(p, k):
            return p_own.at[h, zs[p] * 4 + k]

        def send(ref, i, to):
            push(ref, r2.at[h, i], ds_sem, dr_sem, 2 + 6 * h + i, to)

        def wait(i):
            landed(r2.at[h, i], ds_sem, dr_sem, 2 + 6 * h + i)

        send(slab(0, b2), 0, b_left)
        send(slab(1, b2), 1, b_right)
        send(slab(1, b3), 3, b_left)
        send(slab(0, b1), 4, b_right)
        yield
        for i, p, k, to, j in ((0, 0, b3, b_left, 2), (1, 1, b1, b_right, 5)):
            wait(i)
            ref = slab(p, k)
            ref[...] = (ref[...].astype(F32) + r2[h, i].astype(F32)).astype(BF16)
            send(ref, j, to)
        yield
        for i in (3, 4, 2, 5):
            wait(i)
        for p in (1, 0):
            total = (
                p_own[h, zs[p] * 4 + b].astype(F32) + r2[h, 2 + p].astype(F32) + r2[h, 4 + p].astype(F32)
            )
            for av in range(4):
                for q in range(4):
                    qf[av, q * 4 : q * 4 + 4, :] = total[av * 4 : av * 4 + 4, q * 896 : (q + 1) * 896]
            qb[h, p] = qf[...].astype(BF16)
            for k in (1, 3, 2):
                push(
                    qb.at[h, p, ak[k]], r1.at[h, p, k - 1], ds_sem, dr_sem, 13 + 6 * h + 3 * p + k, a_other[k]
                )
        yield
        sums = []
        for p in (1, 0):
            total = qb[h, p, a].astype(F32)
            for k in (1, 3, 2):
                landed(r1.at[h, p, k - 1], ds_sem, dr_sem, 13 + 6 * h + 3 * p + k)
                total = total + r1[h, p, k - 1].astype(F32)
            sums.append(total)
            if p == 1:
                tz[h] = total.astype(BF16)
                push(tz.at[h], got_peer.at[h], ds_sem, dr_sem, 26 + 3 * h, z_peer)
                push(tz.at[h], got_cross.at[h], ds_sem, dr_sem, 27 + 3 * h, cross)
        tp0[h] = sums[1].astype(BF16)
        push(tp0.at[h], got_partner.at[h], ds_sem, dr_sem, 28 + 3 * h, partner)
        t0[h] = sums[1]
        yield
        landed(got_partner.at[h], ds_sem, dr_sem, 28 + 3 * h)
        landed(got_cross.at[h], ds_sem, dr_sem, 27 + 3 * h)
        landed(got_peer.at[h], ds_sem, dr_sem, 26 + 3 * h)
        stayed = hid[h].astype(F32) + (t0[h] + got_peer[h].astype(F32))
        moved = hid_got[h].astype(F32) + (got_partner[h].astype(F32) + got_cross[h].astype(F32))
        row = lax.rem(lax.broadcasted_iota(jnp.int32, (16, 896), 0), 4)
        final = jnp.where(jnp.where(row < 2, swaps[0], swaps[1]) == 1, moved, stayed)
        request = lax.broadcasted_iota(jnp.int32, (4, 896), 0)
        for q in range(4):
            rows = jnp.zeros((4, 896), F32)
            for p in range(4):
                one = jnp.broadcast_to(final[q * 4 + p : q * 4 + p + 1], (4, 896))
                rows = jnp.where(request == assign_ref[p], one, rows)
            out_ref[:, h * 3584 + q * 896 : h * 3584 + (q + 1) * 896] = rows.astype(BF16)
        yield

    def own_hidden(h):
        lane = lax.broadcasted_iota(jnp.int32, (16, 256), 1)
        sub = lax.broadcasted_iota(jnp.int32, (16, 256), 0)
        rows = jnp.zeros((16, 896), F32)
        for q in range(4):
            pick = jnp.where(lane == me * 4 + sub - q * 4, 1.0, 0.0)
            pick = jnp.where((sub >= q * 4) & (sub < q * 4 + 4), pick, 0.0).astype(BF16)
            rows = rows + lax.dot_general(
                pick, features(2 * h + q // 2, q % 2), NT, preferred_element_type=F32
            )
        hid[h] = rows.astype(BF16)
        push(hid.at[h], hid_got.at[h], rs_sem, rr_sem, 16 + h, partner)

    halves = (reduction(0), reduction(1))
    for _ in range(2):
        for half in halves:
            next(half)
    own_hidden(0)
    next(halves[0])
    own_hidden(1)
    next(halves[1])
    for _ in range(2):
        for half in halves:
            next(half)
    for h in range(2):
        landed(hid_got.at[h], rs_sem, rr_sem, 16 + h)
    for half in halves:
        next(half)
    for copy in started:
        copy.wait_send()


def per_device(
    queries, keys, values, lengths, resid, assign, matching, w_out, gain, gate_w, up_w, down_w
):
    smem = pl.BlockSpec(memory_space=pltpu.SMEM)
    vmem = pl.BlockSpec(memory_space=pltpu.VMEM)
    hbm = pl.BlockSpec(memory_space=pl.ANY)
    dma = pltpu.SemaphoreType.DMA
    scratch = (
        ((4, 1024, 256), BF16),
        ((4, 1024, 256), BF16),
        ((COLS, CW), BF16),
        ((FH, D), BF16),
        ((FH, D), BF16),
        ((FH, D), BF16),
        ((4, D), BF16),
        ((1, D), F32),
        ((2, 128, 128), F32),
        ((128, 256), BF16),
        ((128, 256), BF16),
        ((2, 4, 128, 256), BF16),
        ((2, 512, 128), F32),
        ((16, 16, CW), BF16),
        ((64, COLS, 256), BF16),
        ((FH, 256), F32),
        ((FH, 256), F32),
        ((256, FH), BF16),
        ((8, 16, 256), F32),
        ((8, 16, 256), BF16),
        ((8, 16, 256), BF16),
        ((8, 16, 256), BF16),
        ((8, 32, 128), F32),
        ((8, 32, 128), BF16),
        ((8, 32, 128), BF16),
        ((256, 128), F32),
        ((128, 256), F32),
        ((2, 8, 16, D // 2), F32),
        ((2, 8, 16, D // 2), BF16),
        ((2, 8, 16, D // 2), BF16),
        ((2, 8, 16, D // 2), BF16),
        ((2, 6, 16, D // 2), BF16),
        ((4, 16, 896), F32),
        ((2, 2, 4, 16, 896), BF16),
        ((2, 2, 3, 16, 896), BF16),
        ((2, 16, 896), F32),
    ) + (((2, 16, 896), BF16),) * 7
    return pl.pallas_call(
        kernel,
        out_shape=jax.ShapeDtypeStruct((4, D), BF16),
        in_specs=[smem] * 3 + [vmem] + [hbm] * 8,
        out_specs=vmem,
        scratch_shapes=[pltpu.VMEM(shape, dtype) for shape, dtype in scratch]
        + [dma((n,)) for n in (8, 6, 21, 21, 21, 21, 32, 32, 18, 18)],
        compiler_params=pltpu.CompilerParams(
            collective_id=0, has_side_effects=True, vmem_limit_bytes=60 * 1024 * 1024
        ),
    )(
        lengths, assign[0], matching[:, 0, 0], queries, resid, gain[None],
        keys, values, w_out.T, gate_w[0].T, up_w[0].T, down_w[0],
    )


def solution(mesh):
    rows = P(("attn", "grp", "tp"), None)
    cache = P(("attn", "grp", "tp"), None, None)
    placed = (
        rows,
        cache,
        cache,
        P(("attn", "grp", "tp")),
        rows,
        rows,
        P(None, "attn", "tp"),
        P(None, ("attn", "tp")),
        P(),
        P("grp", None, ("attn", "tp")),
        P("grp", None, ("attn", "tp")),
        P("grp", ("attn", "tp"), None),
    )
    return jax.shard_map(
        per_device, mesh=mesh, in_specs=placed, out_specs=rows, check_vma=False
    )
```

time: 723 us -> 95.7 us (0.13)
  blocking collectives: 372 us -> 0 us
  waiting for transfers between devices: 250 us -> 0 us
  Pallas kernels: 0 us -> 94 us
  matrix products: 36.4 us -> 0 us
  local copies, waits for them, and re-layouts: 31.3 us -> 1.46 us
  between operations: 15.4 us -> 0.01 us
  other arithmetic: 10.3 us -> 0 us
    unnamed x1 -> x0, blocking collectives: 372 us -> none
    all_gather x4 -> x0, waiting for transfers between devices: 245 us -> none  [the longest x2 128 us: serve(): piece = lax.all_gather(batch_rows, ('attn', 'tp'), axis=0, tiled=True)]
    pallas_call x0 -> x1, Pallas kernels: none -> 94 us  [per_device(): pl.pallas_call(kernel, out_shape=jax.ShapeDtypeStruct((4, D), BF16), in_s...]
    dot_general x8 -> x0, matrix products: 36.4 us -> none  [the longest x2 20.1 us: serve(): partial_out = jnp.dot(act, down_w[0], preferred_element_type=jnp.float32)]
    unnamed x29 -> x1, local copies, waits for them, and re-layouts: 18.7 us -> 1.46 us
  transfers between devices with their start and end apart: 8 -> 0, of which waited for: 8 -> 0; matrix products, arithmetic and copies ran while one was open for 4% -> 0% of each run, Pallas kernels for 0% -> 0%
where the time goes in v2:
time: 95.7 us; the launch traced here: 95.5 us
  Pallas kernels  94 us (98%)
  local copies, waits for them, and re-layouts  1.46 us (2%)
    pallas_call x1, Pallas kernels, per_device(): pl.pallas_call(kernel, out_shape=jax.ShapeDtypeStruct((4, D), BF16), in_s...  94 us

profile of v2, /device:TPU:0, one launch (start us, length us, event | category | flops | bytes accessed | tf_op | source)
XLA Modules:
  0.0 95.5 jit_solution(18063355365360444790)
XLA Ops:
  0.0 94.0 %shard_map.118 = bf16[4,7168]{1,0:T(4,128)(2,1)} custom-call(s32[4]{0:T(128)} %len_ref.1, s32[4]{0:T(128)} %bitcast.16, s32[2]{0:T(128)} %bitcast.17, bf16[4,8192]{1,0:T(4,128)(2,1)} %q_ref.1, bf16[4,7168]{1,0:T(4,128)(2,1)} %resid_hbm.1, f32[1,7168]{1,0:T(1,128)} %bitcast.15, bf16[4,1024,256]{2,1,0:T(8,128)(2,1)} %k_hbm.1, bf16[4,1024,256]{2,1,0:T(8,128)(2,1)} %v_hbm.1, ...), custom_call_target="tpu_custom_call" | custom-call | tf_op jit(solution)/shard_map/pallas_call | solution.py:480
  94.0 1.5 %copy.14 = bf16[4,7168]{1,0:T(4,128)(2,1)} copy(bf16[4,7168]{1,0:T(4,128)(2,1)} %shard_map.118) | data formatting | bytes 114688

commit v3 on v2

--- a/solution.py
+++ b/solution.py
@@ -18,10 +18,10 @@
 def kernel(
     len_ref, assign_ref, match_ref, q_ref, resid_hbm, gain_hbm, k_hbm, v_hbm, wo_hbm, g_hbm, u_hbm, d_hbm,
     out_ref,
-    kc, vc, wo, wg, wu, wd, resid_ref, gain_ref,
-    qs, own_b, got_b, cb, sf, ctx_all, ht, acc_g, acc_u, act_s,
+    kc, vc, wo, wg, wu, wg2, wu2, wd, resid_ref, gain_ref,
+    qs, own_b, got_b, cb, sf, ctx_all, ht, acc_g, acc_u, squares, act_out, act_in,
     s1f, s1, s1_got, t1, uf, ub, vb, wf, wt,
-    pf, p_send, p_sib, p_own, r2, qf, qb, r1, t0, tp0, tz, got_peer, got_partner, got_cross, hid, hid_got,
+    p_own, r2, qf, qb, r1, t0, tp0, tz, got_peer, got_partner, got_cross, hid, hid_got,
     kv_sem, w_sem, bs_sem, br_sem, cs_sem, cr_sem, ds_sem, dr_sem, rs_sem, rr_sem,
 ):
     attn, grp, tp = lax.axis_index("attn"), lax.axis_index("grp"), lax.axis_index("tp")
@@ -50,7 +50,7 @@
     loads = [
         pltpu.make_async_copy(src, dst, w_sem.at[i])
         for i, (src, dst) in enumerate(
-            ((resid_hbm, resid_ref), (gain_hbm, gain_ref), (g_hbm, wg), (u_hbm, wu), (wo_hbm, wo), (d_hbm, wd))
+            ((resid_hbm, resid_ref), (gain_hbm, gain_ref), (g_hbm, wg), (u_hbm, wu), (wo_hbm, wo), (d_hbm, wd.at[pl.ds(0, FH)]))
         )
     ]
     for load in loads:
@@ -106,12 +106,12 @@
         own_b[p * 32 : p * 32 + 32] = chosen.astype(BF16)
     pl.semaphore_wait(barrier, 16)
 
-    def gather(block, part, other, s_sem, r_sem, ready):
+    def gather(block, part, other, s_sem, r_sem, ready, base=0):
         def send(ref, i, to):
-            push(ref, ref, s_sem, r_sem, i, to)
+            push(ref, ref, s_sem, r_sem, base + i, to)
 
         def wait(ref, i):
-            landed(ref, s_sem, r_sem, i)
+            landed(ref, s_sem, r_sem, base + i)
 
         def ring_1(p):
             for k in (1, 3, 2):
@@ -159,6 +159,7 @@
         yield
 
     me = ((c * 2 + z) * 4 + b) * 4 + a
+    me_row = ((z * 4 + b) * 4 + a) * 4
 
     def residual():
         loads[0].wait()
@@ -220,17 +221,23 @@
             loads[i].wait()
 
         def scale(i, _):
-            cols = pl.ds(pl.multiple_of(i * 512, 512), 512)
-            by = gain_ref[:, cols]
-            wg[:, cols] = (wg[:, cols].astype(F32) * by).astype(BF16)
-            wu[:, cols] = (wu[:, cols].astype(F32) * by).astype(BF16)
+            rows = pl.ds(pl.multiple_of(i * 16, 16), 16)
+            for src, dst in ((wg, wg2), (wu, wu2)):
+                wide = (src[rows, :].astype(F32) * gain_ref[...]).astype(BF16)
+                for cv in range(2):
+                    for xv in range(4):
+                        first = [xv * 1792 + (zv * 8 + yv * 2 + cv) * COLS for zv in range(2) for yv in range(4)]
+                        dst[cv, rows, xv * 896 : (xv + 1) * 896] = jnp.concatenate(
+                            [wide[:, f : f + COLS] for f in first], axis=1
+                        )
             return 0
 
-        for first, last in ((0, 5), (5, 10), (10, 14)):
-            lax.fori_loop(first, last, scale, 0)
+        for part in range(3):
+            lax.fori_loop(part * 6, part * 6 + 6, scale, 0)
             yield
 
     push(own_b, got_b, rs_sem, rr_sem, 0, partner)
+    push(d_hbm, wd.at[pl.ds(FH, FH)], rs_sem, rr_sem, 18, sibling)
     residual_steps, scaling_steps = residual(), scaling()
     next(residual_steps)
     row = lax.broadcasted_iota(jnp.int32, (128, 256), 0)
@@ -277,62 +284,82 @@
 
         total = lax.fori_loop(0, CW // 1024, step, jnp.zeros((COLS, 128), F32))
         lanes = pl.ds(pl.multiple_of(plane * 128, 128), 128)
-        ht[me, :, lanes] = (wt[:COLS, lanes] + total).astype(BF16)
+        ht[plane, me] = (wt[:COLS, lanes] + total).astype(BF16)
+
+    def gather_hidden(i):
+        half = (c, co)[i]
+        return gather(
+            lambda p, av: ht.at[half, ((c * 2 + zs[p]) * 4 + b) * 4 + av],
+            lambda p, bv: ht.at[half, pl.ds(((c * 2 + zs[p]) * 4 + bv) * 4, 4)],
+            lambda zv, bv: ht.at[(co, c)[i], pl.ds(((co * 2 + zv) * 4 + bv) * 4, 4)],
+            cs_sem,
+            cr_sem,
+            lambda p: None,
+            21 * i,
+        )
+
+    early, late = gather_hidden(0), gather_hidden(1)
+
+    def features(plane, half, xv):
+        parts = []
+        for zv in range(2):
+            for yv in range(4):
+                bv, av = yv * (1 - plane) + xv * plane, xv * (1 - plane) + yv * plane
+                parts.append(ht[half, ((plane * 2 + zv) * 4 + bv) * 4 + av])
+        return jnp.concatenate(parts, axis=0)
+
+    def expand(plane, i):
+        half = (c, co)[i]
+
+        def step(xv, total):
+            cols = pl.ds(pl.multiple_of(xv * 896, 128), 896)
+            part = features(plane, half, xv)
+            acc_g[i] += jnp.dot(wg2[plane, :, cols], part, preferred_element_type=F32)
+            acc_u[i] += jnp.dot(wu2[plane, :, cols], part, preferred_element_type=F32)
+            wide = part.astype(F32)
+            return total + jnp.sum((wide * wide).reshape(112, 8, 128), axis=0)
+
+        squares[i] += lax.fori_loop(0, 4, step, jnp.zeros((8, 128), F32))
+
+    def activate(i):
+        factor = lax.rsqrt(jnp.sum(squares[i], axis=0, keepdims=True) * (1.0 / D) + 1e-5)
+        gate = acc_g[i] * factor
+        act = gate / (1.0 + jnp.exp(-gate)) * (acc_u[i] * factor)
+        return act.T.astype(BF16)
 
     project(c)
+    next(early)
     next(steps)
     project(co)
-
-    steps = gather(
-        lambda p, av: ht.at[((c * 2 + zs[p]) * 4 + b) * 4 + av],
-        lambda p, bv: ht.at[pl.ds(((c * 2 + zs[p]) * 4 + bv) * 4, 4)],
-        lambda zv, bv: ht.at[pl.ds(((co * 2 + zv) * 4 + bv) * 4, 4)],
-        cs_sem,
-        cr_sem,
-        lambda p: None,
-    )
-    for _ in range(7):
-        next(steps)
-
-    def features(xv, zv):
-        parts = []
-        for yv in range(4):
-            parts.append(ht[(zv * 4 + yv) * 4 + xv])
-            parts.append(ht[((2 + zv) * 4 + xv) * 4 + yv])
-        return jnp.concatenate(parts, axis=0)
-
+    next(late)
     acc_g[...] = jnp.zeros_like(acc_g)
     acc_u[...] = jnp.zeros_like(acc_u)
-
-    def expand(i, squares):
-        cols = pl.ds(pl.multiple_of(i * 896, 128), 896)
-        part = features(i // 2, lax.rem(i, 2))
-        acc_g[...] += jnp.dot(wg[:, cols], part, preferred_element_type=F32)
-        acc_u[...] += jnp.dot(wu[:, cols], part, preferred_element_type=F32)
-        wide = part.astype(F32)
-        return squares + jnp.sum((wide * wide).reshape(112, 8, 256), axis=0)
-
-    squares = lax.fori_loop(0, 8, expand, jnp.zeros((8, 256), F32))
-    factor = lax.rsqrt(jnp.sum(squares, axis=0, keepdims=True) * (1.0 / D) + 1e-5)
-    gate = acc_g[...] * factor
-    act = gate / (1.0 + jnp.exp(-gate)) * (acc_u[...] * factor)
-    act_s[...] = act.T.astype(BF16)
-
+    squares[...] = jnp.zeros_like(squares)
+    for _ in range(4):
+        next(early)
+        next(late)
+    next(early)
+    expand(c, 0)
+    next(late)
+    next(early)
+    expand(co, 1)
+    expand(c, 1)
+    act_out[...] = activate(1)
+    push(act_out, act_in, rs_sem, rr_sem, 19, sibling)
+    next(late)
+    expand(co, 0)
+
+    act_own = activate(0)
     loads[5].wait()
-    lhs = jnp.concatenate(
-        [act_s[pl.ds(pl.multiple_of(k * 128, 128), 128), :] for k in (co, c)], axis=0
-    )
+    landed(wd.at[pl.ds(FH, FH)], rs_sem, rr_sem, 18)
+    landed(act_in, rs_sem, rr_sem, 19)
+    lhs = jnp.concatenate([act_own, act_in[...]], axis=1)
 
     def reduction(h):
         for j in range(2):
             cols = pl.ds(j * 1792, 1792)
             part = jnp.dot(lhs, wd[:, pl.ds(h * 3584 + j * 1792, 1792)], preferred_element_type=F32)
-            p_send[h, :, :, cols] = part[:128].astype(BF16).reshape(8, 16, 1792)
-            pf[h, :, :, cols] = part[128:].reshape(8, 16, 1792)
-        push(p_send.at[h], p_sib.at[h], ds_sem, dr_sem, h, sibling)
-        yield
-        landed(p_sib.at[h], ds_sem, dr_sem, h)
-        p_own[h] = (pf[h] + p_sib[h].astype(F32)).astype(BF16)
+            p_own[h, :, :, cols] = part.astype(BF16).reshape(8, 16, 1792)
 
         def slab(p, k):
             return p_own.at[h, zs[p] * 4 + k]
@@ -401,22 +428,26 @@
         yield
 
     def own_hidden(h):
-        lane = lax.broadcasted_iota(jnp.int32, (16, 256), 1)
-        sub = lax.broadcasted_iota(jnp.int32, (16, 256), 0)
+        lane = lax.broadcasted_iota(jnp.int32, (16, 128), 1)
+        sub = lax.broadcasted_iota(jnp.int32, (16, 128), 0)
         rows = jnp.zeros((16, 896), F32)
         for q in range(4):
-            pick = jnp.where(lane == me * 4 + sub - q * 4, 1.0, 0.0)
+            pick = jnp.where(lane == me_row + sub - q * 4, 1.0, 0.0)
             pick = jnp.where((sub >= q * 4) & (sub < q * 4 + 4), pick, 0.0).astype(BF16)
+            xv, zv = 2 * h + q // 2, q % 2
+            parts = []
+            for yv in range(4):
+                parts.append(ht[c, (zv * 4 + yv) * 4 + xv])
+                parts.append(ht[c, ((2 + zv) * 4 + xv) * 4 + yv])
             rows = rows + lax.dot_general(
-                pick, features(2 * h + q // 2, q % 2), NT, preferred_element_type=F32
+                pick, jnp.concatenate(parts, axis=0), NT, preferred_element_type=F32
             )
         hid[h] = rows.astype(BF16)
         push(hid.at[h], hid_got.at[h], rs_sem, rr_sem, 16 + h, partner)
 
     halves = (reduction(0), reduction(1))
-    for _ in range(2):
-        for half in halves:
-            next(half)
+    for half in halves:
+        next(half)
     own_hidden(0)
     next(halves[0])
     own_hidden(1)
@@ -445,7 +476,9 @@
         ((COLS, CW), BF16),
         ((FH, D), BF16),
         ((FH, D), BF16),
-        ((FH, D), BF16),
+        ((2, FH, D // 2), BF16),
+        ((2, FH, D // 2), BF16),
+        ((2 * FH, D), BF16),
         ((4, D), BF16),
         ((1, D), F32),
         ((2, 128, 128), F32),
@@ -454,10 +487,12 @@
         ((2, 4, 128, 256), BF16),
         ((2, 512, 128), F32),
         ((16, 16, CW), BF16),
-        ((64, COLS, 256), BF16),
-        ((FH, 256), F32),
-        ((FH, 256), F32),
-        ((256, FH), BF16),
+        ((2, 64, COLS, 128), BF16),
+        ((2, FH, 128), F32),
+        ((2, FH, 128), F32),
+        ((2, 8, 128), F32),
+        ((128, FH), BF16),
+        ((128, FH), BF16),
         ((8, 16, 256), F32),
         ((8, 16, 256), BF16),
         ((8, 16, 256), BF16),
@@ -467,9 +502,6 @@
         ((8, 32, 128), BF16),
         ((256, 128), F32),
         ((128, 256), F32),
-        ((2, 8, 16, D // 2), F32),
-        ((2, 8, 16, D // 2), BF16),
-        ((2, 8, 16, D // 2), BF16),
         ((2, 8, 16, D // 2), BF16),
         ((2, 6, 16, D // 2), BF16),
         ((4, 16, 896), F32),
@@ -483,7 +515,7 @@
         in_specs=[smem] * 3 + [vmem] + [hbm] * 8,
         out_specs=vmem,
         scratch_shapes=[pltpu.VMEM(shape, dtype) for shape, dtype in scratch]
-        + [dma((n,)) for n in (8, 6, 21, 21, 21, 21, 32, 32, 18, 18)],
+        + [dma((n,)) for n in (8, 6, 21, 21, 42, 42, 32, 32, 20, 20)],
         compiler_params=pltpu.CompilerParams(
             collective_id=0, has_side_effects=True, vmem_limit_bytes=60 * 1024 * 1024
         ),

time: 95.7 us -> 90.1 us (0.941)
  Pallas kernels: 94 us -> 88.4 us
    pallas_call x1, Pallas kernels: 94 us -> 88.4 us  [per_device(): pl.pallas_call(kernel, out_shape=jax.ShapeDtypeStruct((4, D), BF16), in_s...]
where the time goes in v3:
time: 90.1 us; the launch traced here: 89.9 us
  Pallas kernels  88.4 us (98%)
  local copies, waits for them, and re-layouts  1.46 us (2%)
    pallas_call x1, Pallas kernels, per_device(): pl.pallas_call(kernel, out_shape=jax.ShapeDtypeStruct((4, D), BF16), in_s...  88.4 us

profile of v3, /device:TPU:0, one launch (start us, length us, event | category | flops | bytes accessed | tf_op | source)
XLA Modules:
  0.0 89.9 jit_solution(203386677880694951)
XLA Ops:
  0.0 88.4 %shard_map.118 = bf16[4,7168]{1,0:T(4,128)(2,1)} custom-call(s32[4]{0:T(128)} %len_ref.1, s32[4]{0:T(128)} %bitcast.16, s32[2]{0:T(128)} %bitcast.17, bf16[4,8192]{1,0:T(4,128)(2,1)} %q_ref.1, bf16[4,7168]{1,0:T(4,128)(2,1)} %resid_hbm.1, f32[1,7168]{1,0:T(1,128)} %bitcast.15, bf16[4,1024,256]{2,1,0:T(8,128)(2,1)} %k_hbm.1, bf16[4,1024,256]{2,1,0:T(8,128)(2,1)} %v_hbm.1, ...), custom_call_target="tpu_custom_call" | custom-call | tf_op jit(solution)/shard_map/pallas_call | solution.py:512
  88.4 1.5 %copy.14 = bf16[4,7168]{1,0:T(4,128)(2,1)} copy(bf16[4,7168]{1,0:T(4,128)(2,1)} %shard_map.118) | data formatting | bytes 114688

commit v4 on v3

--- a/solution.py
+++ b/solution.py
@@ -28,14 +28,14 @@
     x, z, y, c = attn // 2, lax.rem(attn, 2), tp // 2, lax.rem(tp, 2)
     zo, co = 1 - z, 1 - c
     zs = (z, zo)
-    a = x * co + y * c
-    b = y * co + x * c
+    a = y * co + x * c
+    b = x * co + y * c
 
     def dev(x_, z_, y_, c_):
         return (lax.rem(x_, 4) * 2 + z_, grp, lax.rem(y_, 4) * 2 + c_)
 
-    a_other = [dev(x + k * co, z, y + k * c, c) for k in range(4)]
-    b_right, b_left = dev(x + c, z, y + co, c), dev(x + 3 * c, z, y + 3 * co, c)
+    a_other = [dev(x + k * c, z, y + k * co, c) for k in range(4)]
+    b_right, b_left = dev(x + co, z, y + c, c), dev(x + 3 * co, z, y + 3 * c, c)
     z_peer, sibling = dev(x, zo, y, c), dev(x, z, y, co)
     partner = (attn, 1 - grp, tp)
     cross = (x * 2 + zo, 1 - grp, tp)
@@ -210,7 +210,7 @@
             part = vb[t].astype(F32)
             for n in range(8):
                 plane, zv = t % 2, n % 2
-                bv, av = (n // 2, t // 2) if plane else (t // 2, n // 2)
+                bv, av = (t // 2, n // 2) if plane else (n // 2, t // 2)
                 place = (((plane * 2 + zv) * 4 + bv) * 4 + av) * 4
                 wf[place : place + 4, :] = part[n * 4 : n * 4 + 4]
         wt[...] = wf[...].T
@@ -304,7 +304,7 @@
         parts = []
         for zv in range(2):
             for yv in range(4):
-                bv, av = yv * (1 - plane) + xv * plane, xv * (1 - plane) + yv * plane
+                bv, av = xv * (1 - plane) + yv * plane, yv * (1 - plane) + xv * plane
                 parts.append(ht[half, ((plane * 2 + zv) * 4 + bv) * 4 + av])
         return jnp.concatenate(parts, axis=0)
 
@@ -437,8 +437,8 @@
             xv, zv = 2 * h + q // 2, q % 2
             parts = []
             for yv in range(4):
-                parts.append(ht[c, (zv * 4 + yv) * 4 + xv])
-                parts.append(ht[c, ((2 + zv) * 4 + xv) * 4 + yv])
+                parts.append(ht[c, (zv * 4 + xv) * 4 + yv])
+                parts.append(ht[c, ((2 + zv) * 4 + yv) * 4 + xv])
             rows = rows + lax.dot_general(
                 pick, jnp.concatenate(parts, axis=0), NT, preferred_element_type=F32
             )

time: 90.1 us -> 90.2 us (level)
  no operation moved by 1% of the time
where the time goes in v4:
time: 90.2 us; the launch traced here: 90 us
  Pallas kernels  88.5 us (98%)
  local copies, waits for them, and re-layouts  1.46 us (2%)
    pallas_call x1, Pallas kernels, per_device(): pl.pallas_call(kernel, out_shape=jax.ShapeDtypeStruct((4, D), BF16), in_s...  88.5 us

profile of v4, /device:TPU:0, one launch (start us, length us, event | category | flops | bytes accessed | tf_op | source)
XLA Modules:
  0.0 90.0 jit_solution(10558972673681617769)
XLA Ops:
  0.0 88.5 %shard_map.118 = bf16[4,7168]{1,0:T(4,128)(2,1)} custom-call(s32[4]{0:T(128)} %len_ref.1, s32[4]{0:T(128)} %bitcast.16, s32[2]{0:T(128)} %bitcast.17, bf16[4,8192]{1,0:T(4,128)(2,1)} %q_ref.1, bf16[4,7168]{1,0:T(4,128)(2,1)} %resid_hbm.1, f32[1,7168]{1,0:T(1,128)} %bitcast.15, bf16[4,1024,256]{2,1,0:T(8,128)(2,1)} %k_hbm.1, bf16[4,1024,256]{2,1,0:T(8,128)(2,1)} %v_hbm.1, ...), custom_call_target="tpu_custom_call" | custom-call | tf_op jit(solution)/shard_map/pallas_call | solution.py:512
  88.5 1.5 %copy.14 = bf16[4,7168]{1,0:T(4,128)(2,1)} copy(bf16[4,7168]{1,0:T(4,128)(2,1)} %shard_map.118) | data formatting | bytes 114688

commit v5 on v3

--- a/solution.py
+++ b/solution.py
@@ -19,7 +19,7 @@
     len_ref, assign_ref, match_ref, q_ref, resid_hbm, gain_hbm, k_hbm, v_hbm, wo_hbm, g_hbm, u_hbm, d_hbm,
     out_ref,
     kc, vc, wo, wg, wu, wg2, wu2, wd, resid_ref, gain_ref,
-    qs, own_b, got_b, cb, sf, ctx_all, ht, acc_g, acc_u, squares, act_out, act_in,
+    qs, own_b, got_b, ctx_raw, sf, ctx_all, ht, acc_g, acc_u, squares, act_out, act_in,
     s1f, s1, s1_got, t1, uf, ub, vb, wf, wt,
     p_own, r2, qf, qb, r1, t0, tp0, tz, got_peer, got_partner, got_cross, hid, hid_got,
     kv_sem, w_sem, bs_sem, br_sem, cs_sem, cr_sem, ds_sem, dr_sem, rs_sem, rr_sem,
@@ -40,7 +40,8 @@
     partner = (attn, 1 - grp, tp)
     cross = (x * 2 + zo, 1 - grp, tp)
     ak = [lax.rem(a + k, 4) for k in range(4)]
-    b1, b2, b3 = lax.rem(b + 1, 4), lax.rem(b + 2, 4), lax.rem(b + 3, 4)
+    bk = [lax.rem(b + k, 4) for k in range(4)]
+    b1, b2, b3 = bk[1:]
 
     fetch = []
     for r in range(4):
@@ -106,56 +107,83 @@
         own_b[p * 32 : p * 32 + 32] = chosen.astype(BF16)
     pl.semaphore_wait(barrier, 16)
 
-    def gather(block, part, other, s_sem, r_sem, ready, base=0):
+    def gather(block, slab, other, s_sem, r_sem, base=0):
         def send(ref, i, to):
             push(ref, ref, s_sem, r_sem, base + i, to)
 
         def wait(ref, i):
             landed(ref, s_sem, r_sem, base + i)
 
-        def ring_1(p):
+        def along(p, j):
+            ways = ((0, b_right), (1, b_left))
+            for way, to in ways if j in (0, 3) else ways[::-1]:
+                send(block(p, 0, j), 7 + (p * 4 + j) * 2 + way, to)
+
+        def onward(p, j):
+            if j in (0, 3):
+                wait(block(p, 3, j), 7 + (p * 4 + j) * 2)
+                send(block(p, 3, j), 23 + p * 4 + j, b_right)
+            else:
+                wait(block(p, 1, j), 7 + (p * 4 + j) * 2 + 1)
+                send(block(p, 1, j), 23 + p * 4 + j, b_left)
+
+        def rest(p):
+            for j in (0, 3, 1, 2):
+                if j in (0, 3):
+                    wait(block(p, 1, j), 7 + (p * 4 + j) * 2 + 1)
+                else:
+                    wait(block(p, 3, j), 7 + (p * 4 + j) * 2)
+            across(p, 3)
+            across(p, 1)
+
+        def across(p, k):
+            send(slab(p, k), 31 + p * 4 + k, sibling)
+
+        def first_ring(p):
             for k in (1, 3, 2):
-                send(block(p, a), 3 * p + k, a_other[k])
-
-        def ring_2(p):
-            for k in (1, 3, 2):
-                wait(block(p, ak[4 - k]), 3 * p + k)
-            ready(p)
-            first, second = ((7, b_right), (8, b_left)) if p == 0 else ((10, b_left), (9, b_right))
-            send(part(p, b), *first)
-            send(part(p, b), *second)
-            send(part(p, b), 13 + p, sibling)
-
-        ring_1(0)
-        send(block(0, a), 0, z_peer)
-        yield
-        ring_2(0)
-        wait(block(1, a), 0)
-        ring_1(1)
-        yield
-        ring_2(1)
-        yield
-        wait(part(0, b3), 7)
-        send(part(0, b3), 11, b_right)
-        send(part(0, b3), 15, sibling)
-        wait(part(0, b1), 8)
-        send(part(0, b1), 16, sibling)
-        yield
-        wait(part(1, b1), 10)
-        send(part(1, b1), 12, b_left)
-        send(part(1, b1), 17, sibling)
-        wait(part(1, b3), 9)
-        send(part(1, b3), 18, sibling)
-        yield
-        wait(part(0, b2), 11)
-        send(part(0, b2), 19, sibling)
-        wait(part(1, b2), 12)
-        send(part(1, b2), 20, sibling)
-        yield
-        for i, (zv, k) in enumerate(
-            ((z, 0), (zo, 0), (z, 3), (z, 1), (zo, 1), (zo, 3), (z, 2), (zo, 2))
-        ):
-            wait(other(zv, ak[k]), 13 + i)
+                send(block(p, 0, 0), 3 * p + k, a_other[k])
+
+        def arrive(p, j):
+            wait(block(p, 0, j), 3 * p + 4 - j)
+            along(p, j)
+
+        send(block(0, 0, 0), 0, z_peer)
+        along(0, 0)
+        first_ring(0)
+        yield
+        arrive(0, 3)
+        arrive(0, 1)
+        yield
+        onward(0, 0)
+        wait(block(1, 0, 0), 0)
+        first_ring(1)
+        along(1, 0)
+        arrive(0, 2)
+        across(0, 0)
+        yield
+        onward(0, 3)
+        onward(0, 1)
+        yield
+        onward(0, 2)
+        arrive(1, 3)
+        arrive(1, 1)
+        onward(1, 0)
+        arrive(1, 2)
+        across(1, 0)
+        yield
+        rest(0)
+        yield
+        for j in (3, 1, 2):
+            onward(1, j)
+        rest(1)
+        yield
+        for p in range(2):
+            for j in (0, 3, 1, 2):
+                wait(block(p, 2, j), 23 + p * 4 + j)
+            across(p, 2)
+        yield
+        for p, k in ((0, 0), (1, 0), (0, 3), (0, 1), (1, 3), (1, 1), (0, 2), (1, 2)):
+            wait(other(p, k), 31 + p * 4 + k)
         yield
 
     me = ((c * 2 + z) * 4 + b) * 4 + a
@@ -242,25 +270,35 @@
     next(residual_steps)
     row = lax.broadcasted_iota(jnp.int32, (128, 256), 0)
     landed(got_b, rs_sem, rr_sem, 0)
-    cb[z, a] = jnp.where(jnp.where(row < 64, swaps[0], swaps[1]) == 1, got_b[...], own_b[...])
-
-    def ready(p):
+    ctx_raw[(c * 2 + z) * 4 + b, a] = jnp.where(
+        jnp.where(row < 64, swaps[0], swaps[1]) == 1, got_b[...], own_b[...]
+    )
+
+    def in_rows(place):
         for half in range(2):
-            sf[half] = cb[zs[p], :, :, half * 128 : (half + 1) * 128].astype(F32).reshape(512, 128)
+            sf[half] = ctx_raw[place, :, :, half * 128 : (half + 1) * 128].astype(F32).reshape(512, 128)
         for h in range(32):
             for half in range(2):
                 first = h * 256 + half * 128
-                ctx_all[(c * 2 + zs[p]) * 4 + b, :, first : first + 128] = sf[
-                    half, pl.ds(h, 16, stride=32), :
-                ].astype(BF16)
+                ctx_all[place, :, first : first + 128] = sf[half, pl.ds(h, 16, stride=32), :].astype(BF16)
+
+    def own_rows(*spots):
+        def step(i, _):
+            p, k = spots[0][0], spots[0][1]
+            if len(spots) > 1:
+                p = jnp.where(i == 0, p, spots[1][0])
+                k = jnp.where(i == 0, k, spots[1][1])
+            in_rows((c * 2 + (z + p) % 2) * 4 + lax.rem(b + k, 4))
+            return 0
+
+        lax.fori_loop(0, len(spots), step, 0)
 
     steps = gather(
-        lambda p, av: cb.at[zs[p], av],
-        lambda p, bv: ctx_all.at[(c * 2 + zs[p]) * 4 + bv],
-        lambda zv, bv: ctx_all.at[(co * 2 + zv) * 4 + bv],
+        lambda p, k, j: ctx_raw.at[(c * 2 + zs[p]) * 4 + bk[k], ak[j]],
+        lambda p, k: ctx_raw.at[(c * 2 + zs[p]) * 4 + bk[k]],
+        lambda p, k: ctx_raw.at[(co * 2 + zs[p]) * 4 + ak[k]],
         bs_sem,
         br_sem,
-        ready,
     )
     next(steps)
     next(residual_steps)
@@ -268,12 +306,18 @@
     next(scaling_steps)
     next(steps)
     next(residual_steps)
+    next(steps)
     next(scaling_steps)
     next(steps)
+    own_rows((0, 0), (1, 0))
+    next(steps)
     next(scaling_steps)
-    next(steps)
     next(residual_steps)
-    next(steps)
+    own_rows((0, 3), (0, 1))
+    next(steps)
+    own_rows((1, 3), (1, 1))
+    next(steps)
+    own_rows((0, 2), (1, 2))
     loads[4].wait()
 
     def project(plane):
@@ -289,13 +333,12 @@
     def gather_hidden(i):
         half = (c, co)[i]
         return gather(
-            lambda p, av: ht.at[half, ((c * 2 + zs[p]) * 4 + b) * 4 + av],
-            lambda p, bv: ht.at[half, pl.ds(((c * 2 + zs[p]) * 4 + bv) * 4, 4)],
-            lambda zv, bv: ht.at[(co, c)[i], pl.ds(((co * 2 + zv) * 4 + bv) * 4, 4)],
+            lambda p, k, j: ht.at[half, ((c * 2 + zs[p]) * 4 + bk[k]) * 4 + ak[j]],
+            lambda p, k: ht.at[half, pl.ds(((c * 2 + zs[p]) * 4 + bk[k]) * 4, 4)],
+            lambda p, k: ht.at[(co, c)[i], pl.ds(((co * 2 + zs[p]) * 4 + ak[k]) * 4, 4)],
             cs_sem,
             cr_sem,
-            lambda p: None,
-            21 * i,
+            39 * i,
         )
 
     early, late = gather_hidden(0), gather_hidden(1)
@@ -330,12 +373,13 @@
     project(c)
     next(early)
     next(steps)
+    lax.fori_loop(co * 8, co * 8 + 8, lambda i, _: (in_rows(i), 0)[1], 0)
     project(co)
     next(late)
     acc_g[...] = jnp.zeros_like(acc_g)
     acc_u[...] = jnp.zeros_like(acc_u)
     squares[...] = jnp.zeros_like(squares)
-    for _ in range(4):
+    for _ in range(6):
         next(early)
         next(late)
     next(early)
@@ -484,7 +528,7 @@
         ((2, 128, 128), F32),
         ((128, 256), BF16),
         ((128, 256), BF16),
-        ((2, 4, 128, 256), BF16),
+        ((16, 4, 128, 256), BF16),
         ((2, 512, 128), F32),
         ((16, 16, CW), BF16),
         ((2, 64, COLS, 128), BF16),
@@ -515,7 +559,7 @@
         in_specs=[smem] * 3 + [vmem] + [hbm] * 8,
         out_specs=vmem,
         scratch_shapes=[pltpu.VMEM(shape, dtype) for shape, dtype in scratch]
-        + [dma((n,)) for n in (8, 6, 21, 21, 42, 42, 32, 32, 20, 20)],
+        + [dma((n,)) for n in (8, 6, 39, 39, 78, 78, 32, 32, 20, 20)],
         compiler_params=pltpu.CompilerParams(
             collective_id=0, has_side_effects=True, vmem_limit_bytes=60 * 1024 * 1024
         ),

time: 90.1 us -> 88.5 us (0.982)
  Pallas kernels: 88.4 us -> 86.3 us
    pallas_call x1, Pallas kernels: 88.4 us -> 86.3 us  [per_device(): pl.pallas_call(kernel, out_shape=jax.ShapeDtypeStruct((4, D), BF16), in_s...]
where the time goes in v5:
time: 88.5 us; the launch traced here: 87.8 us
  Pallas kernels  86.3 us (98%)
  local copies, waits for them, and re-layouts  1.46 us (2%)
    pallas_call x1, Pallas kernels, per_device(): pl.pallas_call(kernel, out_shape=jax.ShapeDtypeStruct((4, D), BF16), in_s...  86.3 us

profile of v5, /device:TPU:0, one launch (start us, length us, event | category | flops | bytes accessed | tf_op | source)
XLA Modules:
  0.0 87.8 jit_solution(4336515447979870856)
XLA Ops:
  0.0 86.3 %shard_map.118 = bf16[4,7168]{1,0:T(4,128)(2,1)} custom-call(s32[4]{0:T(128)} %len_ref.1, s32[4]{0:T(128)} %bitcast.16, s32[2]{0:T(128)} %bitcast.17, bf16[4,8192]{1,0:T(4,128)(2,1)} %q_ref.1, bf16[4,7168]{1,0:T(4,128)(2,1)} %resid_hbm.1, f32[1,7168]{1,0:T(1,128)} %bitcast.15, bf16[4,1024,256]{2,1,0:T(8,128)(2,1)} %k_hbm.1, bf16[4,1024,256]{2,1,0:T(8,128)(2,1)} %v_hbm.1, ...), custom_call_target="tpu_custom_call" | custom-call | tf_op jit(solution)/shard_map/pallas_call | solution.py:556
  86.3 1.5 %copy.14 = bf16[4,7168]{1,0:T(4,128)(2,1)} copy(bf16[4,7168]{1,0:T(4,128)(2,1)} %shard_map.118) | data formatting | bytes 114688

commit v6 on v5

--- a/solution.py
+++ b/solution.py
@@ -18,8 +18,8 @@
 def kernel(
     len_ref, assign_ref, match_ref, q_ref, resid_hbm, gain_hbm, k_hbm, v_hbm, wo_hbm, g_hbm, u_hbm, d_hbm,
     out_ref,
-    kc, vc, wo, wg, wu, wg2, wu2, wd, resid_ref, gain_ref,
-    qs, own_b, got_b, ctx_raw, sf, ctx_all, ht, acc_g, acc_u, squares, act_out, act_in,
+    kc, vc, wo, wg, wu, wd, resid_ref, gain_ref,
+    qs, own_b, got_b, ctx_raw, sf, ctx_all, ht, acc_g, acc_u, squares, act_out, act_in, proj_out, proj_in,
     s1f, s1, s1_got, t1, uf, ub, vb, wf, wt,
     p_own, r2, qf, qb, r1, t0, tp0, tz, got_peer, got_partner, got_cross, hid, hid_got,
     kv_sem, w_sem, bs_sem, br_sem, cs_sem, cr_sem, ds_sem, dr_sem, rs_sem, rr_sem,
@@ -51,7 +51,7 @@
     loads = [
         pltpu.make_async_copy(src, dst, w_sem.at[i])
         for i, (src, dst) in enumerate(
-            ((resid_hbm, resid_ref), (gain_hbm, gain_ref), (g_hbm, wg), (u_hbm, wu), (wo_hbm, wo), (d_hbm, wd.at[pl.ds(0, FH)]))
+            ((resid_hbm, resid_ref), (gain_hbm, gain_ref), (g_hbm, wg), (u_hbm, wu), (wo_hbm, wo.at[pl.ds(0, COLS)]), (d_hbm, wd.at[pl.ds(0, FH)]))
         )
     ]
     for load in loads:
@@ -107,7 +107,7 @@
         own_b[p * 32 : p * 32 + 32] = chosen.astype(BF16)
     pl.semaphore_wait(barrier, 16)
 
-    def gather(block, slab, other, s_sem, r_sem, base=0):
+    def gather(block, slab, other, s_sem, r_sem, base=0, share=True):
         def send(ref, i, to):
             push(ref, ref, s_sem, r_sem, base + i, to)
 
@@ -137,7 +137,8 @@
             across(p, 1)
 
         def across(p, k):
-            send(slab(p, k), 31 + p * 4 + k, sibling)
+            if share:
+                send(slab(p, k), 31 + p * 4 + k, sibling)
 
         def first_ring(p):
             for k in (1, 3, 2):
@@ -182,9 +183,10 @@
                 wait(block(p, 2, j), 23 + p * 4 + j)
             across(p, 2)
         yield
-        for p, k in ((0, 0), (1, 0), (0, 3), (0, 1), (1, 3), (1, 1), (0, 2), (1, 2)):
-            wait(other(p, k), 31 + p * 4 + k)
-        yield
+        for p in range(2):
+            for k in (0, 3, 1, 2):
+                wait(other(p, k), 31 + p * 4 + k)
+            yield
 
     me = ((c * 2 + z) * 4 + b) * 4 + a
     me_row = ((z * 4 + b) * 4 + a) * 4
@@ -249,28 +251,24 @@
             loads[i].wait()
 
         def scale(i, _):
-            rows = pl.ds(pl.multiple_of(i * 16, 16), 16)
-            for src, dst in ((wg, wg2), (wu, wu2)):
-                wide = (src[rows, :].astype(F32) * gain_ref[...]).astype(BF16)
-                for cv in range(2):
-                    for xv in range(4):
-                        first = [xv * 1792 + (zv * 8 + yv * 2 + cv) * COLS for zv in range(2) for yv in range(4)]
-                        dst[cv, rows, xv * 896 : (xv + 1) * 896] = jnp.concatenate(
-                            [wide[:, f : f + COLS] for f in first], axis=1
-                        )
+            cols = pl.ds(pl.multiple_of(i * 512, 512), 512)
+            by = gain_ref[:, cols]
+            wg[:, cols] = (wg[:, cols].astype(F32) * by).astype(BF16)
+            wu[:, cols] = (wu[:, cols].astype(F32) * by).astype(BF16)
             return 0
 
-        for part in range(3):
-            lax.fori_loop(part * 6, part * 6 + 6, scale, 0)
+        for first, last in ((0, 3), (3, 6), (6, 10), (10, 14)):
+            lax.fori_loop(first, last, scale, 0)
             yield
 
     push(own_b, got_b, rs_sem, rr_sem, 0, partner)
+    push(wo_hbm, wo.at[pl.ds(COLS, COLS)], rs_sem, rr_sem, 20, sibling)
     push(d_hbm, wd.at[pl.ds(FH, FH)], rs_sem, rr_sem, 18, sibling)
     residual_steps, scaling_steps = residual(), scaling()
     next(residual_steps)
     row = lax.broadcasted_iota(jnp.int32, (128, 256), 0)
     landed(got_b, rs_sem, rr_sem, 0)
-    ctx_raw[(c * 2 + z) * 4 + b, a] = jnp.where(
+    ctx_raw[z * 4 + b, a] = jnp.where(
         jnp.where(row < 64, swaps[0], swaps[1]) == 1, got_b[...], own_b[...]
     )
 
@@ -288,17 +286,18 @@
             if len(spots) > 1:
                 p = jnp.where(i == 0, p, spots[1][0])
                 k = jnp.where(i == 0, k, spots[1][1])
-            in_rows((c * 2 + (z + p) % 2) * 4 + lax.rem(b + k, 4))
+            in_rows(lax.rem(z + p, 2) * 4 + lax.rem(b + k, 4))
             return 0
 
         lax.fori_loop(0, len(spots), step, 0)
 
     steps = gather(
-        lambda p, k, j: ctx_raw.at[(c * 2 + zs[p]) * 4 + bk[k], ak[j]],
-        lambda p, k: ctx_raw.at[(c * 2 + zs[p]) * 4 + bk[k]],
-        lambda p, k: ctx_raw.at[(co * 2 + zs[p]) * 4 + ak[k]],
+        lambda p, k, j: ctx_raw.at[zs[p] * 4 + bk[k], ak[j]],
+        lambda p, k: ctx_raw.at[zs[p] * 4 + bk[k]],
+        None,
         bs_sem,
         br_sem,
+        share=False,
     )
     next(steps)
     next(residual_steps)
@@ -314,21 +313,24 @@
     next(scaling_steps)
     next(residual_steps)
     own_rows((0, 3), (0, 1))
+    next(scaling_steps)
     next(steps)
     own_rows((1, 3), (1, 1))
     next(steps)
     own_rows((0, 2), (1, 2))
     loads[4].wait()
 
-    def project(plane):
+    def project():
         def step(i, acc):
             cols = pl.ds(pl.multiple_of(i * 1024, 1024), 1024)
-            rows = ctx_all[pl.ds(plane * 8, 8), :, cols].reshape(128, 1024)
+            rows = ctx_all[:, :, cols].reshape(128, 1024)
             return acc + lax.dot_general(wo[:, cols], rows, NT, preferred_element_type=F32)
 
-        total = lax.fori_loop(0, CW // 1024, step, jnp.zeros((COLS, 128), F32))
-        lanes = pl.ds(pl.multiple_of(plane * 128, 128), 128)
-        ht[plane, me] = (wt[:COLS, lanes] + total).astype(BF16)
+        return lax.fori_loop(0, CW // 1024, step, jnp.zeros((2 * COLS, 128), F32))
+
+    def hidden_state(half, product):
+        lanes = pl.ds(pl.multiple_of(half * 128, 128), 128)
+        ht[half, me] = (wt[:COLS, lanes] + product).astype(BF16)
 
     def gather_hidden(i):
         half = (c, co)[i]
@@ -343,22 +345,21 @@
 
     early, late = gather_hidden(0), gather_hidden(1)
 
-    def features(plane, half, xv):
+    def features(half, xv, zv):
         parts = []
-        for zv in range(2):
-            for yv in range(4):
-                bv, av = yv * (1 - plane) + xv * plane, xv * (1 - plane) + yv * plane
-                parts.append(ht[half, ((plane * 2 + zv) * 4 + bv) * 4 + av])
+        for yv in range(4):
+            parts.append(ht[half, (zv * 4 + yv) * 4 + xv])
+            parts.append(ht[half, ((2 + zv) * 4 + xv) * 4 + yv])
         return jnp.concatenate(parts, axis=0)
 
-    def expand(plane, i):
+    def expand(i, p):
         half = (c, co)[i]
 
         def step(xv, total):
-            cols = pl.ds(pl.multiple_of(xv * 896, 128), 896)
-            part = features(plane, half, xv)
-            acc_g[i] += jnp.dot(wg2[plane, :, cols], part, preferred_element_type=F32)
-            acc_u[i] += jnp.dot(wu2[plane, :, cols], part, preferred_element_type=F32)
+            cols = pl.ds(pl.multiple_of((xv * 2 + zs[p]) * 896, 128), 896)
+            part = features(half, xv, zs[p])
+            acc_g[i] += jnp.dot(wg[:, cols], part, preferred_element_type=F32)
+            acc_u[i] += jnp.dot(wu[:, cols], part, preferred_element_type=F32)
             wide = part.astype(F32)
             return total + jnp.sum((wide * wide).reshape(112, 8, 128), axis=0)
 
@@ -370,28 +371,33 @@
         act = gate / (1.0 + jnp.exp(-gate)) * (acc_u[i] * factor)
         return act.T.astype(BF16)
 
-    project(c)
+    landed(wo.at[pl.ds(COLS, COLS)], rs_sem, rr_sem, 20)
+    product = project()
+    hidden_state(c, product[:COLS])
     next(early)
-    next(steps)
-    lax.fori_loop(co * 8, co * 8 + 8, lambda i, _: (in_rows(i), 0)[1], 0)
-    project(co)
-    next(late)
+    proj_out[...] = product[COLS:]
+    push(proj_out, proj_in, rs_sem, rr_sem, 21, sibling)
     acc_g[...] = jnp.zeros_like(acc_g)
     acc_u[...] = jnp.zeros_like(acc_u)
     squares[...] = jnp.zeros_like(squares)
+    next(early)
+    landed(proj_in, rs_sem, rr_sem, 21)
+    hidden_state(co, proj_in[...])
+    next(late)
     for _ in range(6):
         next(early)
         next(late)
-    next(early)
-    expand(c, 0)
     next(late)
     next(early)
-    expand(co, 1)
-    expand(c, 1)
+    expand(1, 0)
+    next(early)
+    expand(1, 1)
     act_out[...] = activate(1)
     push(act_out, act_in, rs_sem, rr_sem, 19, sibling)
     next(late)
-    expand(co, 0)
+    expand(0, 0)
+    next(late)
+    expand(0, 1)
 
     act_own = activate(0)
     loads[5].wait()
@@ -479,13 +485,7 @@
             pick = jnp.where(lane == me_row + sub - q * 4, 1.0, 0.0)
             pick = jnp.where((sub >= q * 4) & (sub < q * 4 + 4), pick, 0.0).astype(BF16)
             xv, zv = 2 * h + q // 2, q % 2
-            parts = []
-            for yv in range(4):
-                parts.append(ht[c, (zv * 4 + yv) * 4 + xv])
-                parts.append(ht[c, ((2 + zv) * 4 + xv) * 4 + yv])
-            rows = rows + lax.dot_general(
-                pick, jnp.concatenate(parts, axis=0), NT, preferred_element_type=F32
-            )
+            rows = rows + lax.dot_general(pick, features(c, xv, zv), NT, preferred_element_type=F32)
         hid[h] = rows.astype(BF16)
         push(hid.at[h], hid_got.at[h], rs_sem, rr_sem, 16 + h, partner)
 
@@ -517,26 +517,26 @@
     scratch = (
         ((4, 1024, 256), BF16),
         ((4, 1024, 256), BF16),
-        ((COLS, CW), BF16),
+        ((2 * COLS, CW), BF16),
         ((FH, D), BF16),
         ((FH, D), BF16),
-        ((2, FH, D // 2), BF16),
-        ((2, FH, D // 2), BF16),
         ((2 * FH, D), BF16),
         ((4, D), BF16),
         ((1, D), F32),
         ((2, 128, 128), F32),
         ((128, 256), BF16),
         ((128, 256), BF16),
-        ((16, 4, 128, 256), BF16),
+        ((8, 4, 128, 256), BF16),
         ((2, 512, 128), F32),
-        ((16, 16, CW), BF16),
+        ((8, 16, CW), BF16),
         ((2, 64, COLS, 128), BF16),
         ((2, FH, 128), F32),
         ((2, FH, 128), F32),
         ((2, 8, 128), F32),
         ((128, FH), BF16),
         ((128, FH), BF16),
+        ((COLS, 128), F32),
+        ((COLS, 128), F32),
         ((8, 16, 256), F32),
         ((8, 16, 256), BF16),
         ((8, 16, 256), BF16),
@@ -559,7 +559,7 @@
         in_specs=[smem] * 3 + [vmem] + [hbm] * 8,
         out_specs=vmem,
         scratch_shapes=[pltpu.VMEM(shape, dtype) for shape, dtype in scratch]
-        + [dma((n,)) for n in (8, 6, 39, 39, 78, 78, 32, 32, 20, 20)],
+        + [dma((n,)) for n in (8, 6, 31, 31, 78, 78, 32, 32, 22, 22)],
         compiler_params=pltpu.CompilerParams(
             collective_id=0, has_side_effects=True, vmem_limit_bytes=60 * 1024 * 1024
         ),

time: 88.5 us -> 90.9 us (1.027)
  Pallas kernels: 86.3 us -> 89.2 us
    pallas_call x1, Pallas kernels: 86.3 us -> 89.2 us  [per_device(): pl.pallas_call(kernel, out_shape=jax.ShapeDtypeStruct((4, D), BF16), in_s...]
where the time goes in v6:
time: 90.9 us; the launch traced here: 90.7 us
  Pallas kernels  89.2 us (98%)
  local copies, waits for them, and re-layouts  1.46 us (2%)
    pallas_call x1, Pallas kernels, per_device(): pl.pallas_call(kernel, out_shape=jax.ShapeDtypeStruct((4, D), BF16), in_s...  89.2 us

profile of v6, /device:TPU:0, one launch (start us, length us, event | category | flops | bytes accessed | tf_op | source)
XLA Modules:
  0.0 90.7 jit_solution(2781563314523823097)
XLA Ops:
  0.0 89.2 %shard_map.118 = bf16[4,7168]{1,0:T(4,128)(2,1)} custom-call(s32[4]{0:T(128)} %len_ref.1, s32[4]{0:T(128)} %bitcast.16, s32[2]{0:T(128)} %bitcast.17, bf16[4,8192]{1,0:T(4,128)(2,1)} %q_ref.1, bf16[4,7168]{1,0:T(4,128)(2,1)} %resid_hbm.1, f32[1,7168]{1,0:T(1,128)} %bitcast.15, bf16[4,1024,256]{2,1,0:T(8,128)(2,1)} %k_hbm.1, bf16[4,1024,256]{2,1,0:T(8,128)(2,1)} %v_hbm.1, ...), custom_call_target="tpu_custom_call" | custom-call | tf_op jit(solution)/shard_map/pallas_call | solution.py:556
  89.2 1.5 %copy.14 = bf16[4,7168]{1,0:T(4,128)(2,1)} copy(bf16[4,7168]{1,0:T(4,128)(2,1)} %shard_map.118) | data formatting | bytes 114688

commit v7 on v6

--- a/solution.py
+++ b/solution.py
@@ -19,7 +19,7 @@
     len_ref, assign_ref, match_ref, q_ref, resid_hbm, gain_hbm, k_hbm, v_hbm, wo_hbm, g_hbm, u_hbm, d_hbm,
     out_ref,
     kc, vc, wo, wg, wu, wd, resid_ref, gain_ref,
-    qs, own_b, got_b, ctx_raw, sf, ctx_all, ht, acc_g, acc_u, squares, act_out, act_in, proj_out, proj_in,
+    qs, own_b, got_b, ctx_raw, sf, ctx_all, ht, acc_g, acc_u, squares, proj_out, proj_in, p_send, p_sib,
     s1f, s1, s1_got, t1, uf, ub, vb, wf, wt,
     p_own, r2, qf, qb, r1, t0, tp0, tz, got_peer, got_partner, got_cross, hid, hid_got,
     kv_sem, w_sem, bs_sem, br_sem, cs_sem, cr_sem, ds_sem, dr_sem, rs_sem, rr_sem,
@@ -51,12 +51,9 @@
     loads = [
         pltpu.make_async_copy(src, dst, w_sem.at[i])
         for i, (src, dst) in enumerate(
-            ((resid_hbm, resid_ref), (gain_hbm, gain_ref), (g_hbm, wg), (u_hbm, wu), (wo_hbm, wo.at[pl.ds(0, COLS)]), (d_hbm, wd.at[pl.ds(0, FH)]))
+            ((resid_hbm, resid_ref), (gain_hbm, gain_ref), (g_hbm, wg), (u_hbm, wu), (wo_hbm, wo.at[pl.ds(0, COLS)]), (d_hbm, wd))
         )
     ]
-    for load in loads:
-        load.start()
-
     barrier = pltpu.get_barrier_semaphore()
     others = [partner, cross]
     for k in range(1, 8):
@@ -99,13 +96,19 @@
         fetch[2 * r + 1].wait()
         return jnp.dot(probs, vc[r], preferred_element_type=F32)
 
-    contexts = [attend(r) for r in range(4)]
+    contexts = [attend(0)]
+    for load in loads:
+        load.start()
+    contexts.append(attend(1))
+    pl.semaphore_wait(barrier, 16)
+    push(wo_hbm, wo.at[pl.ds(COLS, COLS)], rs_sem, rr_sem, 20, sibling)
+    contexts.append(attend(2))
+    contexts.append(attend(3))
     for p in range(4):
         chosen = contexts[0]
         for r in range(1, 4):
             chosen = jnp.where(assign_ref[p] == r, contexts[r], chosen)
         own_b[p * 32 : p * 32 + 32] = chosen.astype(BF16)
-    pl.semaphore_wait(barrier, 16)
 
     def gather(block, slab, other, s_sem, r_sem, base=0, share=True):
         def send(ref, i, to):
@@ -262,8 +265,6 @@
             yield
 
     push(own_b, got_b, rs_sem, rr_sem, 0, partner)
-    push(wo_hbm, wo.at[pl.ds(COLS, COLS)], rs_sem, rr_sem, 20, sibling)
-    push(d_hbm, wd.at[pl.ds(FH, FH)], rs_sem, rr_sem, 18, sibling)
     residual_steps, scaling_steps = residual(), scaling()
     next(residual_steps)
     row = lax.broadcasted_iota(jnp.int32, (128, 256), 0)
@@ -392,24 +393,28 @@
     expand(1, 0)
     next(early)
     expand(1, 1)
-    act_out[...] = activate(1)
-    push(act_out, act_in, rs_sem, rr_sem, 19, sibling)
+    loads[5].wait()
+    act = activate(1)
+    for h in range(2):
+        for j in range(2):
+            cols = pl.ds(j * 1792, 1792)
+            part = jnp.dot(act, wd[:, pl.ds(h * 3584 + j * 1792, 1792)], preferred_element_type=F32)
+            p_send[h, :, :, cols] = part.astype(BF16).reshape(8, 16, 1792)
+        push(p_send.at[h], p_sib.at[h], ds_sem, dr_sem, h, sibling)
     next(late)
     expand(0, 0)
     next(late)
     expand(0, 1)
 
     act_own = activate(0)
-    loads[5].wait()
-    landed(wd.at[pl.ds(FH, FH)], rs_sem, rr_sem, 18)
-    landed(act_in, rs_sem, rr_sem, 19)
-    lhs = jnp.concatenate([act_own, act_in[...]], axis=1)
 
     def reduction(h):
+        landed(p_sib.at[h], ds_sem, dr_sem, h)
         for j in range(2):
             cols = pl.ds(j * 1792, 1792)
-            part = jnp.dot(lhs, wd[:, pl.ds(h * 3584 + j * 1792, 1792)], preferred_element_type=F32)
-            p_own[h, :, :, cols] = part.astype(BF16).reshape(8, 16, 1792)
+            part = jnp.dot(act_own, wd[:, pl.ds(h * 3584 + j * 1792, 1792)], preferred_element_type=F32)
+            part = part.reshape(8, 16, 1792) + p_sib[h, :, :, cols].astype(F32)
+            p_own[h, :, :, cols] = part.astype(BF16)
 
         def slab(p, k):
             return p_own.at[h, zs[p] * 4 + k]
@@ -520,7 +525,7 @@
         ((2 * COLS, CW), BF16),
         ((FH, D), BF16),
         ((FH, D), BF16),
-        ((2 * FH, D), BF16),
+        ((FH, D), BF16),
         ((4, D), BF16),
         ((1, D), F32),
         ((2, 128, 128), F32),
@@ -533,10 +538,10 @@
         ((2, FH, 128), F32),
         ((2, FH, 128), F32),
         ((2, 8, 128), F32),
-        ((128, FH), BF16),
-        ((128, FH), BF16),
         ((COLS, 128), F32),
         ((COLS, 128), F32),
+        ((2, 8, 16, D // 2), BF16),
+        ((2, 8, 16, D // 2), BF16),
         ((8, 16, 256), F32),
         ((8, 16, 256), BF16),
         ((8, 16, 256), BF16),

time: 90.9 us -> 91.8 us (level)
  no operation moved by 1% of the time
where the time goes in v7:
time: 91.8 us; the launch traced here: 91.6 us
  Pallas kernels  90.1 us (98%)
  local copies, waits for them, and re-layouts  1.46 us (2%)
    pallas_call x1, Pallas kernels, per_device(): pl.pallas_call(kernel, out_shape=jax.ShapeDtypeStruct((4, D), BF16), in_s...  90.1 us

profile of v7, /device:TPU:0, one launch (start us, length us, event | category | flops | bytes accessed | tf_op | source)
XLA Modules:
  0.0 91.6 jit_solution(18327651073851104816)
XLA Ops:
  0.0 90.1 %shard_map.118 = bf16[4,7168]{1,0:T(4,128)(2,1)} custom-call(s32[4]{0:T(128)} %len_ref.1, s32[4]{0:T(128)} %bitcast.16, s32[2]{0:T(128)} %bitcast.17, bf16[4,8192]{1,0:T(4,128)(2,1)} %q_ref.1, bf16[4,7168]{1,0:T(4,128)(2,1)} %resid_hbm.1, f32[1,7168]{1,0:T(1,128)} %bitcast.15, bf16[4,1024,256]{2,1,0:T(8,128)(2,1)} %k_hbm.1, bf16[4,1024,256]{2,1,0:T(8,128)(2,1)} %v_hbm.1, ...), custom_call_target="tpu_custom_call" | custom-call | tf_op jit(solution)/shard_map/pallas_call | solution.py:561
  90.1 1.5 %copy.14 = bf16[4,7168]{1,0:T(4,128)(2,1)} copy(bf16[4,7168]{1,0:T(4,128)(2,1)} %shard_map.118) | data formatting | bytes 114688

commit v8 on v3

--- a/solution.py
+++ b/solution.py
@@ -20,7 +20,7 @@
     out_ref,
     kc, vc, wo, wg, wu, wg2, wu2, wd, resid_ref, gain_ref,
     qs, own_b, got_b, cb, sf, ctx_all, ht, acc_g, acc_u, squares, act_out, act_in,
-    s1f, s1, s1_got, t1, uf, ub, vb, wf, wt,
+    s1f, s1, s1_got, t1, uf, ub, vb, wf, wt, turned, lhs_f,
     p_own, r2, qf, qb, r1, t0, tp0, tz, got_peer, got_partner, got_cross, hid, hid_got,
     kv_sem, w_sem, bs_sem, br_sem, cs_sem, cr_sem, ds_sem, dr_sem, rs_sem, rr_sem,
 ):
@@ -28,19 +28,23 @@
     x, z, y, c = attn // 2, lax.rem(attn, 2), tp // 2, lax.rem(tp, 2)
     zo, co = 1 - z, 1 - c
     zs = (z, zo)
-    a = x * co + y * c
-    b = y * co + x * c
-
     def dev(x_, z_, y_, c_):
         return (lax.rem(x_, 4) * 2 + z_, grp, lax.rem(y_, 4) * 2 + c_)
 
-    a_other = [dev(x + k * co, z, y + k * c, c) for k in range(4)]
-    b_right, b_left = dev(x + c, z, y + co, c), dev(x + 3 * c, z, y + 3 * co, c)
     z_peer, sibling = dev(x, zo, y, c), dev(x, z, y, co)
     partner = (attn, 1 - grp, tp)
     cross = (x * 2 + zo, 1 - grp, tp)
-    ak = [lax.rem(a + k, 4) for k in range(4)]
-    b1, b2, b3 = lax.rem(b + 1, 4), lax.rem(b + 2, 4), lax.rem(b + 3, 4)
+
+    def axes(e):
+        a, b = x * (1 - e) + y * e, y * (1 - e) + x * e
+        return (
+            [lax.rem(a + k, 4) for k in range(4)],
+            [lax.rem(b + k, 4) for k in range(4)],
+            [dev(x + k * (1 - e), z, y + k * e, c) for k in range(4)],
+            [dev(x + k * e, z, y + k * (1 - e), c) for k in range(4)],
+        )
+
+    ways = (axes(c), axes(co))
 
     fetch = []
     for r in range(4):
@@ -103,10 +107,15 @@
         chosen = contexts[0]
         for r in range(1, 4):
             chosen = jnp.where(assign_ref[p] == r, contexts[r], chosen)
-        own_b[p * 32 : p * 32 + 32] = chosen.astype(BF16)
+        for hh in range(2):
+            own_b[hh * 64 + p * 16 : hh * 64 + p * 16 + 16] = chosen[hh * 16 : hh * 16 + 16].astype(BF16)
     pl.semaphore_wait(barrier, 16)
 
-    def gather(block, part, other, s_sem, r_sem, ready, base=0):
+    def gather(way, block, part, other, s_sem, r_sem, ready, base):
+        ak, bk, a_other, b_other = way
+        a, (b, b1, b2, b3) = ak[0], bk
+        b_right, b_left = b_other[1], b_other[3]
+
         def send(ref, i, to):
             push(ref, ref, s_sem, r_sem, base + i, to)
 
@@ -158,7 +167,8 @@
             wait(other(zv, ak[k]), 13 + i)
         yield
 
-    me = ((c * 2 + z) * 4 + b) * 4 + a
+    a, b = ways[0][0][0], ways[0][1][0]
+    me = (((c * 2 + z) * 4 + b) * 4 + a, ((c * 2 + z) * 4 + a) * 4 + b)
     me_row = ((z * 4 + b) * 4 + a) * 4
 
     def residual():
@@ -232,8 +242,8 @@
                         )
             return 0
 
-        for part in range(3):
-            lax.fori_loop(part * 6, part * 6 + 6, scale, 0)
+        for part in range(6):
+            lax.fori_loop(part * 3, part * 3 + 3, scale, 0)
             yield
 
     push(own_b, got_b, rs_sem, rr_sem, 0, partner)
@@ -242,54 +252,84 @@
     next(residual_steps)
     row = lax.broadcasted_iota(jnp.int32, (128, 256), 0)
     landed(got_b, rs_sem, rr_sem, 0)
-    cb[z, a] = jnp.where(jnp.where(row < 64, swaps[0], swaps[1]) == 1, got_b[...], own_b[...])
-
-    def ready(p):
-        for half in range(2):
-            sf[half] = cb[zs[p], :, :, half * 128 : (half + 1) * 128].astype(F32).reshape(512, 128)
-        for h in range(32):
+    served = jnp.where(jnp.where(row % 64 < 32, swaps[0], swaps[1]) == 1, got_b[...], own_b[...])
+    for hh in range(2):
+        cb[hh, z, ways[hh][0][0]] = served[hh * 64 : hh * 64 + 64]
+
+    def gather_context(hh):
+        way = ways[hh]
+
+        def ready(p):
             for half in range(2):
-                first = h * 256 + half * 128
-                ctx_all[(c * 2 + zs[p]) * 4 + b, :, first : first + 128] = sf[
-                    half, pl.ds(h, 16, stride=32), :
-                ].astype(BF16)
-
-    steps = gather(
-        lambda p, av: cb.at[zs[p], av],
-        lambda p, bv: ctx_all.at[(c * 2 + zs[p]) * 4 + bv],
-        lambda zv, bv: ctx_all.at[(co * 2 + zv) * 4 + bv],
-        bs_sem,
-        br_sem,
-        ready,
-    )
-    next(steps)
-    next(residual_steps)
-    next(steps)
-    next(scaling_steps)
-    next(steps)
+                sf[half] = cb[hh, zs[p], :, :, half * 128 : (half + 1) * 128].astype(F32).reshape(256, 128)
+            for h in range(16):
+                for half in range(2):
+                    first = h * 256 + half * 128
+                    ctx_all[hh, (c * 2 + zs[p]) * 4 + way[1][0], :, first : first + 128] = sf[
+                        half, pl.ds(h, 16, stride=16), :
+                    ].astype(BF16)
+
+        return gather(
+            way,
+            lambda p, av: cb.at[hh, zs[p], av],
+            lambda p, bv: ctx_all.at[hh, (c * 2 + zs[p]) * 4 + bv],
+            lambda zv, bv: ctx_all.at[hh, (co * 2 + zv) * 4 + bv],
+            bs_sem,
+            br_sem,
+            ready,
+            21 * hh,
+        )
+
+    steps = (gather_context(0), gather_context(1))
+
+    def both(pair):
+        for one in pair:
+            next(one)
+
+    both(steps)
     next(residual_steps)
     next(scaling_steps)
-    next(steps)
+    both(steps)
     next(scaling_steps)
-    next(steps)
+    both(steps)
     next(residual_steps)
-    next(steps)
+    next(scaling_steps)
+    both(steps)
+    next(scaling_steps)
+    both(steps)
+    next(scaling_steps)
+    next(residual_steps)
+    next(scaling_steps)
+    both(steps)
     loads[4].wait()
 
     def project(plane):
-        def step(i, acc):
+        def rows(hh, cols):
+            return ctx_all[hh, pl.ds(plane * 8, 8), :, cols].reshape(128, 1024)
+
+        def step(i, sums):
             cols = pl.ds(pl.multiple_of(i * 1024, 1024), 1024)
-            rows = ctx_all[pl.ds(plane * 8, 8), :, cols].reshape(128, 1024)
-            return acc + lax.dot_general(wo[:, cols], rows, NT, preferred_element_type=F32)
-
-        total = lax.fori_loop(0, CW // 1024, step, jnp.zeros((COLS, 128), F32))
+            last = pl.ds(pl.multiple_of(i * 1024 + CW // 2, 1024), 1024)
+            one = lax.dot_general(wo[:, cols], rows(0, cols), NT, preferred_element_type=F32)
+            two = lax.dot_general(rows(1, cols), wo[:, last], NT, preferred_element_type=F32)
+            return sums[0] + one, sums[1] + two
+
+        one, two = lax.fori_loop(
+            0, CW // 2048, step, (jnp.zeros((COLS, 128), F32), jnp.zeros((128, COLS), F32))
+        )
+        for zv in range(2):
+            for i in range(4):
+                for j in range(4):
+                    src, dst = ((zv * 4 + i) * 4 + j) * 4, ((zv * 4 + j) * 4 + i) * 4
+                    turned[dst : dst + 4, :COLS] = two[src : src + 4]
         lanes = pl.ds(pl.multiple_of(plane * 128, 128), 128)
-        ht[plane, me] = (wt[:COLS, lanes] + total).astype(BF16)
+        return (wt[:COLS, lanes] + (one + turned[...].T[:COLS])).astype(BF16)
 
     def gather_hidden(i):
         half = (c, co)[i]
         return gather(
-            lambda p, av: ht.at[half, ((c * 2 + zs[p]) * 4 + b) * 4 + av],
+            ways[i],
+            lambda p, av: ht.at[half, ((c * 2 + zs[p]) * 4 + ways[i][1][0]) * 4 + av],
             lambda p, bv: ht.at[half, pl.ds(((c * 2 + zs[p]) * 4 + bv) * 4, 4)],
             lambda zv, bv: ht.at[(co, c)[i], pl.ds(((co * 2 + zv) * 4 + bv) * 4, 4)],
             cs_sem,
@@ -304,7 +344,7 @@
         parts = []
         for zv in range(2):
             for yv in range(4):
-                bv, av = yv * (1 - plane) + xv * plane, xv * (1 - plane) + yv * plane
+                bv, av = yv * (1 - half) + xv * half, xv * (1 - half) + yv * half
                 parts.append(ht[half, ((plane * 2 + zv) * 4 + bv) * 4 + av])
         return jnp.concatenate(parts, axis=0)
 
@@ -327,10 +367,10 @@
         act = gate / (1.0 + jnp.exp(-gate)) * (acc_u[i] * factor)
         return act.T.astype(BF16)
 
-    project(c)
+    ht[c, me[0]] = project(c)
     next(early)
-    next(steps)
-    project(co)
+    both(steps)
+    ht[co, me[1]] = project(co)
     next(late)
     acc_g[...] = jnp.zeros_like(acc_g)
     acc_u[...] = jnp.zeros_like(acc_u)
@@ -354,11 +394,20 @@
     landed(wd.at[pl.ds(FH, FH)], rs_sem, rr_sem, 18)
     landed(act_in, rs_sem, rr_sem, 19)
     lhs = jnp.concatenate([act_own, act_in[...]], axis=1)
+    wide_lhs = lhs.astype(F32)
+    for zv in range(2):
+        for i in range(4):
+            for j in range(4):
+                src, dst = ((zv * 4 + i) * 4 + j) * 4, ((zv * 4 + j) * 4 + i) * 4
+                lhs_f[dst : dst + 4, :] = wide_lhs[src : src + 4]
+    lhs = (lhs, lhs_f[...].astype(BF16))
 
     def reduction(h):
+        ak, (b, b1, b2, b3), a_other, b_other = ways[h]
+        a, b_right, b_left = ak[0], b_other[1], b_other[3]
         for j in range(2):
             cols = pl.ds(j * 1792, 1792)
-            part = jnp.dot(lhs, wd[:, pl.ds(h * 3584 + j * 1792, 1792)], preferred_element_type=F32)
+            part = jnp.dot(lhs[h], wd[:, pl.ds(h * 3584 + j * 1792, 1792)], preferred_element_type=F32)
             p_own[h, :, :, cols] = part.astype(BF16).reshape(8, 16, 1792)
 
         def slab(p, k):
@@ -437,8 +486,9 @@
             xv, zv = 2 * h + q // 2, q % 2
             parts = []
             for yv in range(4):
-                parts.append(ht[c, (zv * 4 + yv) * 4 + xv])
-                parts.append(ht[c, ((2 + zv) * 4 + xv) * 4 + yv])
+                for plane in range(2):
+                    bv, av = yv * co + xv * c, xv * co + yv * c
+                    parts.append(ht[c, ((plane * 2 + zv) * 4 + bv) * 4 + av])
             rows = rows + lax.dot_general(
                 pick, jnp.concatenate(parts, axis=0), NT, preferred_element_type=F32
             )
@@ -484,9 +534,9 @@
         ((2, 128, 128), F32),
         ((128, 256), BF16),
         ((128, 256), BF16),
-        ((2, 4, 128, 256), BF16),
-        ((2, 512, 128), F32),
-        ((16, 16, CW), BF16),
+        ((2, 2, 4, 64, 256), BF16),
+        ((2, 256, 128), F32),
+        ((2, 16, 16, CW // 2), BF16),
         ((2, 64, COLS, 128), BF16),
         ((2, FH, 128), F32),
         ((2, FH, 128), F32),
@@ -502,6 +552,8 @@
         ((8, 32, 128), BF16),
         ((256, 128), F32),
         ((128, 256), F32),
+        ((128, 128), F32),
+        ((128, 2 * FH), F32),
         ((2, 8, 16, D // 2), BF16),
         ((2, 6, 16, D // 2), BF16),
         ((4, 16, 896), F32),
@@ -515,7 +567,7 @@
         in_specs=[smem] * 3 + [vmem] + [hbm] * 8,
         out_specs=vmem,
         scratch_shapes=[pltpu.VMEM(shape, dtype) for shape, dtype in scratch]
-        + [dma((n,)) for n in (8, 6, 21, 21, 42, 42, 32, 32, 20, 20)],
+        + [dma((n,)) for n in (8, 6, 42, 42, 42, 42, 32, 32, 20, 20)],
         compiler_params=pltpu.CompilerParams(
             collective_id=0, has_side_effects=True, vmem_limit_bytes=60 * 1024 * 1024
         ),

time: 90.1 us -> 86.1 us (0.956)
  Pallas kernels: 88.4 us -> 84.4 us
    pallas_call x1, Pallas kernels: 88.4 us -> 84.4 us  [per_device(): pl.pallas_call(kernel, out_shape=jax.ShapeDtypeStruct((4, D), BF16), in_s...]
where the time goes in v8:
time: 86.1 us; the launch traced here: 85.9 us
  Pallas kernels  84.4 us (98%)
  local copies, waits for them, and re-layouts  1.46 us (2%)
    pallas_call x1, Pallas kernels, per_device(): pl.pallas_call(kernel, out_shape=jax.ShapeDtypeStruct((4, D), BF16), in_s...  84.4 us

profile of v8, /device:TPU:0, one launch (start us, length us, event | category | flops | bytes accessed | tf_op | source)
XLA Modules:
  0.0 85.9 jit_solution(7381475971569503025)
XLA Ops:
  0.0 84.4 %shard_map.118 = bf16[4,7168]{1,0:T(4,128)(2,1)} custom-call(s32[4]{0:T(128)} %len_ref.1, s32[4]{0:T(128)} %bitcast.16, s32[2]{0:T(128)} %bitcast.17, bf16[4,8192]{1,0:T(4,128)(2,1)} %q_ref.1, bf16[4,7168]{1,0:T(4,128)(2,1)} %resid_hbm.1, f32[1,7168]{1,0:T(1,128)} %bitcast.15, bf16[4,1024,256]{2,1,0:T(8,128)(2,1)} %k_hbm.1, bf16[4,1024,256]{2,1,0:T(8,128)(2,1)} %v_hbm.1, ...), custom_call_target="tpu_custom_call" | custom-call | tf_op jit(solution)/shard_map/pallas_call | solution.py:564
  84.4 1.5 %copy.14 = bf16[4,7168]{1,0:T(4,128)(2,1)} copy(bf16[4,7168]{1,0:T(4,128)(2,1)} %shard_map.118) | data formatting | bytes 114688

commit v9 on v8

--- a/solution.py
+++ b/solution.py
@@ -16,9 +16,9 @@
 
 
 def kernel(
-    len_ref, assign_ref, match_ref, q_ref, resid_hbm, gain_hbm, k_hbm, v_hbm, wo_hbm, g_hbm, u_hbm, d_hbm,
+    len_ref, assign_ref, match_ref, q_hbm, resid_hbm, gain_hbm, k_hbm, v_hbm, wo_hbm, g_hbm, u_hbm, d_hbm,
     out_ref,
-    kc, vc, wo, wg, wu, wg2, wu2, wd, resid_ref, gain_ref,
+    q_ref, kc, vc, wo, wg, wu, wg2, wu2, wd, resid_ref, gain_ref,
     qs, own_b, got_b, cb, sf, ctx_all, ht, acc_g, acc_u, squares, act_out, act_in,
     s1f, s1, s1_got, t1, uf, ub, vb, wf, wt, turned, lhs_f,
     p_own, r2, qf, qb, r1, t0, tp0, tz, got_peer, got_partner, got_cross, hid, hid_got,
@@ -46,6 +46,8 @@
 
     ways = (axes(c), axes(co))
 
+    q_load = pltpu.make_async_copy(q_hbm, q_ref, w_sem.at[6])
+    q_load.start()
     fetch = []
     for r in range(4):
         for src, dst in ((k_hbm, kc), (v_hbm, vc)):
@@ -57,9 +59,6 @@
             ((resid_hbm, resid_ref), (gain_hbm, gain_ref), (g_hbm, wg), (u_hbm, wu), (wo_hbm, wo), (d_hbm, wd.at[pl.ds(0, FH)]))
         )
     ]
-    for load in loads:
-        load.start()
-
     barrier = pltpu.get_barrier_semaphore()
     others = [partner, cross]
     for k in range(1, 8):
@@ -70,6 +69,10 @@
 
     started = []
 
+    def drain(keep=0):
+        while len(started) > keep:
+            started.pop(0).wait_send()
+
     def push(src, dst, s_sem, r_sem, i, to):
         copy = pltpu.make_async_remote_copy(
             src_ref=src, dst_ref=dst, send_sem=s_sem.at[i], recv_sem=r_sem.at[i],
@@ -84,6 +87,7 @@
             device_id=sibling, device_id_type=MESH,
         ).wait_recv()
 
+    q_load.wait()
     wide_q = q_ref[...].astype(F32)
     for h in range(32):
         for half in range(2):
@@ -102,13 +106,16 @@
         fetch[2 * r + 1].wait()
         return jnp.dot(probs, vc[r], preferred_element_type=F32)
 
-    contexts = [attend(r) for r in range(4)]
+    contexts = [attend(0)]
+    for load in loads:
+        load.start()
+    contexts += [attend(r) for r in range(1, 4)]
     for p in range(4):
         chosen = contexts[0]
         for r in range(1, 4):
             chosen = jnp.where(assign_ref[p] == r, contexts[r], chosen)
         for hh in range(2):
-            own_b[hh * 64 + p * 16 : hh * 64 + p * 16 + 16] = chosen[hh * 16 : hh * 16 + 16].astype(BF16)
+            own_b[hh, p * 16 : p * 16 + 16] = chosen[hh * 16 : hh * 16 + 16].astype(BF16)
     pl.semaphore_wait(barrier, 16)
 
     def gather(way, block, part, other, s_sem, r_sem, ready, base):
@@ -135,8 +142,8 @@
             send(part(p, b), *second)
             send(part(p, b), 13 + p, sibling)
 
+        send(block(0, a), 0, z_peer)
         ring_1(0)
-        send(block(0, a), 0, z_peer)
         yield
         ring_2(0)
         wait(block(1, a), 0)
@@ -246,15 +253,13 @@
             lax.fori_loop(part * 3, part * 3 + 3, scale, 0)
             yield
 
-    push(own_b, got_b, rs_sem, rr_sem, 0, partner)
+    push(own_b.at[0], got_b.at[0], rs_sem, rr_sem, 0, partner)
+    push(own_b.at[1], got_b.at[1], rs_sem, rr_sem, 20, partner)
     push(d_hbm, wd.at[pl.ds(FH, FH)], rs_sem, rr_sem, 18, sibling)
     residual_steps, scaling_steps = residual(), scaling()
     next(residual_steps)
-    row = lax.broadcasted_iota(jnp.int32, (128, 256), 0)
-    landed(got_b, rs_sem, rr_sem, 0)
-    served = jnp.where(jnp.where(row % 64 < 32, swaps[0], swaps[1]) == 1, got_b[...], own_b[...])
-    for hh in range(2):
-        cb[hh, z, ways[hh][0][0]] = served[hh * 64 : hh * 64 + 64]
+    next(scaling_steps)
+    row = lax.broadcasted_iota(jnp.int32, (64, 256), 0)
 
     def gather_context(hh):
         way = ways[hh]
@@ -269,7 +274,11 @@
                         half, pl.ds(h, 16, stride=16), :
                     ].astype(BF16)
 
-        return gather(
+        landed(got_b.at[hh], rs_sem, rr_sem, 20 * hh)
+        cb[hh, z, way[0][0]] = jnp.where(
+            jnp.where(row < 32, swaps[0], swaps[1]) == 1, got_b[hh], own_b[hh]
+        )
+        yield from gather(
             way,
             lambda p, av: cb.at[hh, zs[p], av],
             lambda p, bv: ctx_all.at[hh, (c * 2 + zs[p]) * 4 + bv],
@@ -288,7 +297,6 @@
 
     both(steps)
     next(residual_steps)
-    next(scaling_steps)
     both(steps)
     next(scaling_steps)
     both(steps)
@@ -375,9 +383,12 @@
     acc_g[...] = jnp.zeros_like(acc_g)
     acc_u[...] = jnp.zeros_like(acc_u)
     squares[...] = jnp.zeros_like(squares)
-    for _ in range(4):
+    before = len(started)
+    for i in range(4):
         next(early)
         next(late)
+        if i == 0:
+            drain(len(started) - before)
     next(early)
     expand(c, 0)
     next(late)
@@ -394,20 +405,23 @@
     landed(wd.at[pl.ds(FH, FH)], rs_sem, rr_sem, 18)
     landed(act_in, rs_sem, rr_sem, 19)
     lhs = jnp.concatenate([act_own, act_in[...]], axis=1)
-    wide_lhs = lhs.astype(F32)
-    for zv in range(2):
-        for i in range(4):
-            for j in range(4):
-                src, dst = ((zv * 4 + i) * 4 + j) * 4, ((zv * 4 + j) * 4 + i) * 4
-                lhs_f[dst : dst + 4, :] = wide_lhs[src : src + 4]
-    lhs = (lhs, lhs_f[...].astype(BF16))
+
+    def other_order():
+        wide_lhs = lhs.astype(F32)
+        for zv in range(2):
+            for i in range(4):
+                for j in range(4):
+                    src, dst = ((zv * 4 + i) * 4 + j) * 4, ((zv * 4 + j) * 4 + i) * 4
+                    lhs_f[dst : dst + 4, :] = wide_lhs[src : src + 4]
+        return lhs_f[...].astype(BF16)
 
     def reduction(h):
+        rows = other_order() if h else lhs
         ak, (b, b1, b2, b3), a_other, b_other = ways[h]
         a, b_right, b_left = ak[0], b_other[1], b_other[3]
         for j in range(2):
             cols = pl.ds(j * 1792, 1792)
-            part = jnp.dot(lhs[h], wd[:, pl.ds(h * 3584 + j * 1792, 1792)], preferred_element_type=F32)
+            part = jnp.dot(rows, wd[:, pl.ds(h * 3584 + j * 1792, 1792)], preferred_element_type=F32)
             p_own[h, :, :, cols] = part.astype(BF16).reshape(8, 16, 1792)
 
         def slab(p, k):
@@ -496,9 +510,11 @@
         push(hid.at[h], hid_got.at[h], rs_sem, rr_sem, 16 + h, partner)
 
     halves = (reduction(0), reduction(1))
+    before = len(started)
     for half in halves:
         next(half)
     own_hidden(0)
+    drain(len(started) - before)
     next(halves[0])
     own_hidden(1)
     next(halves[1])
@@ -509,8 +525,7 @@
         landed(hid_got.at[h], rs_sem, rr_sem, 16 + h)
     for half in halves:
         next(half)
-    for copy in started:
-        copy.wait_send()
+    drain()
 
 
 def per_device(
@@ -521,6 +536,7 @@
     hbm = pl.BlockSpec(memory_space=pl.ANY)
     dma = pltpu.SemaphoreType.DMA
     scratch = (
+        ((4, CW), BF16),
         ((4, 1024, 256), BF16),
         ((4, 1024, 256), BF16),
         ((COLS, CW), BF16),
@@ -532,8 +548,8 @@
         ((4, D), BF16),
         ((1, D), F32),
         ((2, 128, 128), F32),
-        ((128, 256), BF16),
-        ((128, 256), BF16),
+        ((2, 64, 256), BF16),
+        ((2, 64, 256), BF16),
         ((2, 2, 4, 64, 256), BF16),
         ((2, 256, 128), F32),
         ((2, 16, 16, CW // 2), BF16),
@@ -564,10 +580,10 @@
     return pl.pallas_call(
         kernel,
         out_shape=jax.ShapeDtypeStruct((4, D), BF16),
-        in_specs=[smem] * 3 + [vmem] + [hbm] * 8,
+        in_specs=[smem] * 3 + [hbm] * 9,
         out_specs=vmem,
         scratch_shapes=[pltpu.VMEM(shape, dtype) for shape, dtype in scratch]
-        + [dma((n,)) for n in (8, 6, 42, 42, 42, 42, 32, 32, 20, 20)],
+        + [dma((n,)) for n in (8, 7, 42, 42, 42, 42, 32, 32, 21, 21)],
         compiler_params=pltpu.CompilerParams(
             collective_id=0, has_side_effects=True, vmem_limit_bytes=60 * 1024 * 1024
         ),

time: 86.1 us -> 84.9 us (0.986)
  Pallas kernels: 84.4 us -> 83.3 us
    pallas_call x1, Pallas kernels: 84.4 us -> 83.3 us  [per_device(): pl.pallas_call(kernel, out_shape=jax.ShapeDtypeStruct((4, D), BF16), in_s...]
where the time goes in v9:
time: 84.9 us; the launch traced here: 84.8 us
  Pallas kernels  83.3 us (98%)
  local copies, waits for them, and re-layouts  1.46 us (2%)
    pallas_call x1, Pallas kernels, per_device(): pl.pallas_call(kernel, out_shape=jax.ShapeDtypeStruct((4, D), BF16), in_s...  83.3 us

profile of v9, /device:TPU:0, one launch (start us, length us, event | category | flops | bytes accessed | tf_op | source)
XLA Modules:
  0.0 84.8 jit_solution(18351933452906554863)
XLA Ops:
  0.0 83.3 %shard_map.118 = bf16[4,7168]{1,0:T(4,128)(2,1)} custom-call(s32[4]{0:T(128)} %len_ref.1, s32[4]{0:T(128)} %bitcast.16, s32[2]{0:T(128)} %bitcast.17, bf16[4,8192]{1,0:T(4,128)(2,1)} %q_hbm.1, bf16[4,7168]{1,0:T(4,128)(2,1)} %resid_hbm.1, f32[1,7168]{1,0:T(1,128)} %bitcast.15, bf16[4,1024,256]{2,1,0:T(8,128)(2,1)} %k_hbm.1, bf16[4,1024,256]{2,1,0:T(8,128)(2,1)} %v_hbm.1, ...), custom_call_target="tpu_custom_call" | custom-call | tf_op jit(solution)/shard_map/pallas_call | solution.py:580
  83.3 1.5 %copy.14 = bf16[4,7168]{1,0:T(4,128)(2,1)} copy(bf16[4,7168]{1,0:T(4,128)(2,1)} %shard_map.118) | data formatting | bytes 114688

commit v10 on v9

--- a/solution.py
+++ b/solution.py
@@ -19,7 +19,7 @@
     len_ref, assign_ref, match_ref, q_hbm, resid_hbm, gain_hbm, k_hbm, v_hbm, wo_hbm, g_hbm, u_hbm, d_hbm,
     out_ref,
     q_ref, kc, vc, wo, wg, wu, wg2, wu2, wd, resid_ref, gain_ref,
-    qs, own_b, got_b, cb, sf, ctx_all, ht, acc_g, acc_u, squares, act_out, act_in,
+    qs, own_b, got_b, cross_b, peer_b, flags, flag_out, flag_in, cb, sf, ctx_all, ht, acc_g, acc_u, squares, act_out, act_in,
     s1f, s1, s1_got, t1, uf, ub, vb, wf, wt, turned, lhs_f,
     p_own, r2, qf, qb, r1, t0, tp0, tz, got_peer, got_partner, got_cross, hid, hid_got,
     kv_sem, w_sem, bs_sem, br_sem, cs_sem, cr_sem, ds_sem, dr_sem, rs_sem, rr_sem,
@@ -49,8 +49,8 @@
     q_load = pltpu.make_async_copy(q_hbm, q_ref, w_sem.at[6])
     q_load.start()
     fetch = []
-    for r in range(4):
-        for src, dst in ((k_hbm, kc), (v_hbm, vc)):
+    for src, dst in ((k_hbm, kc), (v_hbm, vc)):
+        for r in range(4):
             fetch.append(pltpu.make_async_copy(src.at[r], dst.at[r], kv_sem.at[len(fetch)]))
             fetch[-1].start()
     loads = [
@@ -96,20 +96,21 @@
     slot = lax.broadcasted_iota(jnp.int32, (32, 1024), 1)
     swaps = (match_ref[0], match_ref[1])
 
-    def attend(r):
-        fetch[2 * r].wait()
+    def weigh(r):
         query = jnp.concatenate([qs[half, r * 32 : (r + 1) * 32] for half in range(2)], axis=1).astype(BF16)
         scores = lax.dot_general(query, kc[r], NT, preferred_element_type=F32) * (256 ** -0.5)
         scores = jnp.where(slot < len_ref[r], scores, -1e30)
         expo = jnp.exp(scores - jnp.max(scores, axis=-1, keepdims=True))
-        probs = (expo / jnp.sum(expo, axis=-1, keepdims=True)).astype(BF16)
-        fetch[2 * r + 1].wait()
-        return jnp.dot(probs, vc[r], preferred_element_type=F32)
-
-    contexts = [attend(0)]
+        return (expo / jnp.sum(expo, axis=-1, keepdims=True)).astype(BF16)
+
+    for copy in fetch[:4]:
+        copy.wait()
     for load in loads:
         load.start()
-    contexts += [attend(r) for r in range(1, 4)]
+    probs = [weigh(r) for r in range(4)]
+    for copy in fetch[4:]:
+        copy.wait()
+    contexts = [jnp.dot(probs[r], vc[r], preferred_element_type=F32) for r in range(4)]
     for p in range(4):
         chosen = contexts[0]
         for r in range(1, 4):
@@ -118,7 +119,7 @@
             own_b[hh, p * 16 : p * 16 + 16] = chosen[hh * 16 : hh * 16 + 16].astype(BF16)
     pl.semaphore_wait(barrier, 16)
 
-    def gather(way, block, part, other, s_sem, r_sem, ready, base):
+    def gather(way, block, part, other, s_sem, r_sem, ready, base, peer=None):
         ak, bk, a_other, b_other = way
         a, (b, b1, b2, b3) = ak[0], bk
         b_right, b_left = b_other[1], b_other[3]
@@ -142,12 +143,18 @@
             send(part(p, b), *second)
             send(part(p, b), 13 + p, sibling)
 
-        send(block(0, a), 0, z_peer)
+        if peer is None:
+            send(block(0, a), 0, z_peer)
         ring_1(0)
         yield
-        ring_2(0)
-        wait(block(1, a), 0)
-        ring_1(1)
+        if peer is None:
+            ring_2(0)
+            wait(block(1, a), 0)
+            ring_1(1)
+        else:
+            peer()
+            ring_1(1)
+            ring_2(0)
         yield
         ring_2(1)
         yield
@@ -168,11 +175,10 @@
         wait(part(1, b2), 12)
         send(part(1, b2), 20, sibling)
         yield
-        for i, (zv, k) in enumerate(
-            ((z, 0), (zo, 0), (z, 3), (z, 1), (zo, 1), (zo, 3), (z, 2), (zo, 2))
-        ):
-            wait(other(zv, ak[k]), 13 + i)
-        yield
+        for p, spots in enumerate((((13, 0), (15, 3), (16, 1), (19, 2)), ((14, 0), (18, 3), (17, 1), (20, 2)))):
+            for i, k in spots:
+                wait(other(zs[p], ak[k]), i)
+            yield
 
     a, b = ways[0][0][0], ways[0][1][0]
     me = (((c * 2 + z) * 4 + b) * 4 + a, ((c * 2 + z) * 4 + a) * 4 + b)
@@ -243,7 +249,11 @@
                 wide = (src[rows, :].astype(F32) * gain_ref[...]).astype(BF16)
                 for cv in range(2):
                     for xv in range(4):
-                        first = [xv * 1792 + (zv * 8 + yv * 2 + cv) * COLS for zv in range(2) for yv in range(4)]
+                        first = [
+                            ((xv // 2 * 4 + x2 * 2 + xv % 2) * 8 + yv * 2 + cv) * COLS
+                            for x2 in range(2)
+                            for yv in range(4)
+                        ]
                         dst[cv, rows, xv * 896 : (xv + 1) * 896] = jnp.concatenate(
                             [wide[:, f : f + COLS] for f in first], axis=1
                         )
@@ -253,8 +263,15 @@
             lax.fori_loop(part * 3, part * 3 + 3, scale, 0)
             yield
 
-    push(own_b.at[0], got_b.at[0], rs_sem, rr_sem, 0, partner)
-    push(own_b.at[1], got_b.at[1], rs_sem, rr_sem, 20, partner)
+    for m in range(2):
+        flags[m * 8 : m * 8 + 8, :] = jnp.full((8, 128), swaps[m], jnp.int32).astype(F32)
+    flag_out[...] = flags[...].astype(BF16)
+    for hh in range(2):
+        push(own_b.at[hh], got_b.at[hh], rs_sem, rr_sem, 20 * hh, partner)
+    push(flag_out, flag_in, rs_sem, rr_sem, 21, z_peer)
+    for hh in range(2):
+        push(own_b.at[hh], cross_b.at[hh], rs_sem, rr_sem, 22 + hh, cross)
+        push(own_b.at[hh], peer_b.at[hh], rs_sem, rr_sem, 24 + hh, z_peer)
     push(d_hbm, wd.at[pl.ds(FH, FH)], rs_sem, rr_sem, 18, sibling)
     residual_steps, scaling_steps = residual(), scaling()
     next(residual_steps)
@@ -278,6 +295,20 @@
         cb[hh, z, way[0][0]] = jnp.where(
             jnp.where(row < 32, swaps[0], swaps[1]) == 1, got_b[hh], own_b[hh]
         )
+
+        def peer():
+            if hh == 0:
+                landed(flag_in, rs_sem, rr_sem, 21)
+            landed(cross_b.at[hh], rs_sem, rr_sem, 22 + hh)
+            landed(peer_b.at[hh], rs_sem, rr_sem, 24 + hh)
+            wide = flag_in[...].astype(F32)
+            flag = jnp.concatenate(
+                [jnp.broadcast_to(wide[m * 8 : m * 8 + 1], (32, 128)) for m in range(2)], axis=0
+            )
+            flag = jnp.concatenate([flag, flag], axis=1)
+            theirs = jnp.where(flag > 0.5, cross_b[hh].astype(F32), peer_b[hh].astype(F32))
+            cb[hh, zo, way[0][0]] = theirs.astype(BF16)
+
         yield from gather(
             way,
             lambda p, av: cb.at[hh, zs[p], av],
@@ -287,6 +318,7 @@
             br_sem,
             ready,
             21 * hh,
+            peer,
         )
 
     steps = (gather_context(0), gather_context(1))
@@ -348,26 +380,28 @@
 
     early, late = gather_hidden(0), gather_hidden(1)
 
-    def features(plane, half, xv):
+    def features(plane, half, n):
         parts = []
-        for zv in range(2):
+        for x2 in range(2):
             for yv in range(4):
+                xv = n // 2 * 2 + x2
                 bv, av = yv * (1 - half) + xv * half, xv * (1 - half) + yv * half
-                parts.append(ht[half, ((plane * 2 + zv) * 4 + bv) * 4 + av])
+                parts.append(ht[half, ((plane * 2 + lax.rem(n, 2)) * 4 + bv) * 4 + av])
         return jnp.concatenate(parts, axis=0)
 
-    def expand(plane, i):
+    def expand(plane, i, *ps):
         half = (c, co)[i]
 
-        def step(xv, total):
-            cols = pl.ds(pl.multiple_of(xv * 896, 128), 896)
-            part = features(plane, half, xv)
+        def step(k, total):
+            n = (k // len(ps)) * 2 + (zs[ps[0]] if len(ps) == 1 else lax.rem(k, 2))
+            cols = pl.ds(pl.multiple_of(n * 896, 128), 896)
+            part = features(plane, half, n)
             acc_g[i] += jnp.dot(wg2[plane, :, cols], part, preferred_element_type=F32)
             acc_u[i] += jnp.dot(wu2[plane, :, cols], part, preferred_element_type=F32)
             wide = part.astype(F32)
             return total + jnp.sum((wide * wide).reshape(112, 8, 128), axis=0)
 
-        squares[i] += lax.fori_loop(0, 4, step, jnp.zeros((8, 128), F32))
+        squares[i] += lax.fori_loop(0, 2 * len(ps), step, jnp.zeros((8, 128), F32))
 
     def activate(i):
         factor = lax.rsqrt(jnp.sum(squares[i], axis=0, keepdims=True) * (1.0 / D) + 1e-5)
@@ -377,6 +411,7 @@
 
     ht[c, me[0]] = project(c)
     next(early)
+    both(steps)
     both(steps)
     ht[co, me[1]] = project(co)
     next(late)
@@ -390,15 +425,18 @@
         if i == 0:
             drain(len(started) - before)
     next(early)
-    expand(c, 0)
+    expand(c, 0, 0, 1)
     next(late)
     next(early)
-    expand(co, 1)
-    expand(c, 1)
+    next(early)
+    expand(co, 1, 0, 1)
+    expand(c, 1, 0, 1)
     act_out[...] = activate(1)
     push(act_out, act_in, rs_sem, rr_sem, 19, sibling)
     next(late)
-    expand(co, 0)
+    expand(co, 0, 0)
+    next(late)
+    expand(co, 0, 1)
 
     act_own = activate(0)
     loads[5].wait()
@@ -550,6 +588,11 @@
         ((2, 128, 128), F32),
         ((2, 64, 256), BF16),
         ((2, 64, 256), BF16),
+        ((2, 64, 256), BF16),
+        ((2, 64, 256), BF16),
+        ((16, 128), F32),
+        ((16, 128), BF16),
+        ((16, 128), BF16),
         ((2, 2, 4, 64, 256), BF16),
         ((2, 256, 128), F32),
         ((2, 16, 16, CW // 2), BF16),
@@ -583,7 +626,7 @@
         in_specs=[smem] * 3 + [hbm] * 9,
         out_specs=vmem,
         scratch_shapes=[pltpu.VMEM(shape, dtype) for shape, dtype in scratch]
-        + [dma((n,)) for n in (8, 7, 42, 42, 42, 42, 32, 32, 21, 21)],
+        + [dma((n,)) for n in (8, 7, 42, 42, 42, 42, 32, 32, 26, 26)],
         compiler_params=pltpu.CompilerParams(
             collective_id=0, has_side_effects=True, vmem_limit_bytes=60 * 1024 * 1024
         ),

time: 84.9 us -> 82.7 us (0.974)
  Pallas kernels: 83.3 us -> 81.1 us
    pallas_call x1, Pallas kernels: 83.3 us -> 81.1 us  [per_device(): pl.pallas_call(kernel, out_shape=jax.ShapeDtypeStruct((4, D), BF16), in_s...]
where the time goes in v10:
time: 82.7 us; the launch traced here: 82.6 us
  Pallas kernels  81.1 us (98%)
  local copies, waits for them, and re-layouts  1.46 us (2%)
    pallas_call x1, Pallas kernels, per_device(): pl.pallas_call(kernel, out_shape=jax.ShapeDtypeStruct((4, D), BF16), in_s...  81.1 us

profile of v10, /device:TPU:0, one launch (start us, length us, event | category | flops | bytes accessed | tf_op | source)
XLA Modules:
  0.0 82.6 jit_solution(4659092121265377388)
XLA Ops:
  0.0 81.1 %shard_map.118 = bf16[4,7168]{1,0:T(4,128)(2,1)} custom-call(s32[4]{0:T(128)} %len_ref.1, s32[4]{0:T(128)} %bitcast.16, s32[2]{0:T(128)} %bitcast.17, bf16[4,8192]{1,0:T(4,128)(2,1)} %q_hbm.1, bf16[4,7168]{1,0:T(4,128)(2,1)} %resid_hbm.1, f32[1,7168]{1,0:T(1,128)} %bitcast.15, bf16[4,1024,256]{2,1,0:T(8,128)(2,1)} %k_hbm.1, bf16[4,1024,256]{2,1,0:T(8,128)(2,1)} %v_hbm.1, ...), custom_call_target="tpu_custom_call" | custom-call | tf_op jit(solution)/shard_map/pallas_call | solution.py:623
  81.1 1.5 %copy.14 = bf16[4,7168]{1,0:T(4,128)(2,1)} copy(bf16[4,7168]{1,0:T(4,128)(2,1)} %shard_map.118) | data formatting | bytes 114688

commit v11 on v10

--- a/solution.py
+++ b/solution.py
@@ -18,8 +18,8 @@
 def kernel(
     len_ref, assign_ref, match_ref, q_hbm, resid_hbm, gain_hbm, k_hbm, v_hbm, wo_hbm, g_hbm, u_hbm, d_hbm,
     out_ref,
-    q_ref, kc, vc, wo, wg, wu, wg2, wu2, wd, resid_ref, gain_ref,
-    qs, own_b, got_b, cross_b, peer_b, flags, flag_out, flag_in, cb, sf, ctx_all, ht, acc_g, acc_u, squares, act_out, act_in,
+    q_ref, kc, vc, wo, wg, wu, w2, wd, resid_ref, gain_ref,
+    qs, own_b, got_b, cross_b, peer_b, flags, flag_out, flag_in, cb, sf, ctx_all, ht, acc, squares, act_out, act_in,
     s1f, s1, s1_got, t1, uf, ub, vb, wf, wt, turned, lhs_f,
     p_own, r2, qf, qb, r1, t0, tp0, tz, got_peer, got_partner, got_cross, hid, hid_got,
     kv_sem, w_sem, bs_sem, br_sem, cs_sem, cr_sem, ds_sem, dr_sem, rs_sem, rr_sem,
@@ -107,6 +107,8 @@
         copy.wait()
     for load in loads:
         load.start()
+    pl.semaphore_wait(barrier, 16)
+    push(d_hbm, wd.at[pl.ds(FH, FH)], rs_sem, rr_sem, 18, sibling)
     probs = [weigh(r) for r in range(4)]
     for copy in fetch[4:]:
         copy.wait()
@@ -117,7 +119,6 @@
             chosen = jnp.where(assign_ref[p] == r, contexts[r], chosen)
         for hh in range(2):
             own_b[hh, p * 16 : p * 16 + 16] = chosen[hh * 16 : hh * 16 + 16].astype(BF16)
-    pl.semaphore_wait(barrier, 16)
 
     def gather(way, block, part, other, s_sem, r_sem, ready, base, peer=None):
         ak, bk, a_other, b_other = way
@@ -245,7 +246,8 @@
 
         def scale(i, _):
             rows = pl.ds(pl.multiple_of(i * 16, 16), 16)
-            for src, dst in ((wg, wg2), (wu, wu2)):
+            for k, src in enumerate((wg, wu)):
+                spot = pl.ds(pl.multiple_of(k * FH + i * 16, 16), 16)
                 wide = (src[rows, :].astype(F32) * gain_ref[...]).astype(BF16)
                 for cv in range(2):
                     for xv in range(4):
@@ -254,7 +256,7 @@
                             for x2 in range(2)
                             for yv in range(4)
                         ]
-                        dst[cv, rows, xv * 896 : (xv + 1) * 896] = jnp.concatenate(
+                        w2[cv, spot, xv * 896 : (xv + 1) * 896] = jnp.concatenate(
                             [wide[:, f : f + COLS] for f in first], axis=1
                         )
             return 0
@@ -272,7 +274,6 @@
     for hh in range(2):
         push(own_b.at[hh], cross_b.at[hh], rs_sem, rr_sem, 22 + hh, cross)
         push(own_b.at[hh], peer_b.at[hh], rs_sem, rr_sem, 24 + hh, z_peer)
-    push(d_hbm, wd.at[pl.ds(FH, FH)], rs_sem, rr_sem, 18, sibling)
     residual_steps, scaling_steps = residual(), scaling()
     next(residual_steps)
     next(scaling_steps)
@@ -396,8 +397,7 @@
             n = (k // len(ps)) * 2 + (zs[ps[0]] if len(ps) == 1 else lax.rem(k, 2))
             cols = pl.ds(pl.multiple_of(n * 896, 128), 896)
             part = features(plane, half, n)
-            acc_g[i] += jnp.dot(wg2[plane, :, cols], part, preferred_element_type=F32)
-            acc_u[i] += jnp.dot(wu2[plane, :, cols], part, preferred_element_type=F32)
+            acc[i] += jnp.dot(w2[plane, :, cols], part, preferred_element_type=F32)
             wide = part.astype(F32)
             return total + jnp.sum((wide * wide).reshape(112, 8, 128), axis=0)
 
@@ -405,8 +405,8 @@
 
     def activate(i):
         factor = lax.rsqrt(jnp.sum(squares[i], axis=0, keepdims=True) * (1.0 / D) + 1e-5)
-        gate = acc_g[i] * factor
-        act = gate / (1.0 + jnp.exp(-gate)) * (acc_u[i] * factor)
+        gate = acc[i, :FH] * factor
+        act = gate / (1.0 + jnp.exp(-gate)) * (acc[i, FH:] * factor)
         return act.T.astype(BF16)
 
     ht[c, me[0]] = project(c)
@@ -415,8 +415,7 @@
     both(steps)
     ht[co, me[1]] = project(co)
     next(late)
-    acc_g[...] = jnp.zeros_like(acc_g)
-    acc_u[...] = jnp.zeros_like(acc_u)
+    acc[...] = jnp.zeros_like(acc)
     squares[...] = jnp.zeros_like(squares)
     before = len(started)
     for i in range(4):
@@ -580,8 +579,7 @@
         ((COLS, CW), BF16),
         ((FH, D), BF16),
         ((FH, D), BF16),
-        ((2, FH, D // 2), BF16),
-        ((2, FH, D // 2), BF16),
+        ((2, 2 * FH, D // 2), BF16),
         ((2 * FH, D), BF16),
         ((4, D), BF16),
         ((1, D), F32),
@@ -597,8 +595,7 @@
         ((2, 256, 128), F32),
         ((2, 16, 16, CW // 2), BF16),
         ((2, 64, COLS, 128), BF16),
-        ((2, FH, 128), F32),
-        ((2, FH, 128), F32),
+        ((2, 2 * FH, 128), F32),
         ((2, 8, 128), F32),
         ((128, FH), BF16),
         ((128, FH), BF16),
@@ -622,7 +619,7 @@
     ) + (((2, 16, 896), BF16),) * 7
     return pl.pallas_call(
         kernel,
-        out_shape=jax.ShapeDtypeStruct((4, D), BF16),
+        out_shape=pltpu.VMEM((4, D), BF16),
         in_specs=[smem] * 3 + [hbm] * 9,
         out_specs=vmem,
         scratch_shapes=[pltpu.VMEM(shape, dtype) for shape, dtype in scratch]

time: 82.7 us -> 81.9 us (level)
  local copies, waits for them, and re-layouts: 1.46 us -> 0.63 us
    unnamed x1, local copies, waits for them, and re-layouts: 1.46 us -> 0.63 us
where the time goes in v11:
time: 81.9 us; the launch traced here: 81.8 us
  Pallas kernels  81.1 us (99%)
    pallas_call x1, Pallas kernels, per_device(): pl.pallas_call(kernel, out_shape=pltpu.VMEM((4, D), BF16), in_specs=[smem...  81.1 us

profile of v11, /device:TPU:0, one launch (start us, length us, event | category | flops | bytes accessed | tf_op | source)
XLA Modules:
  0.0 81.8 jit_solution(9987535834079785293)
XLA Ops:
  0.0 81.1 %shard_map.118 = bf16[4,7168]{1,0:T(4,128)(2,1)S(1)} custom-call(s32[4]{0:T(128)} %len_ref.1, s32[4]{0:T(128)} %bitcast.16, s32[2]{0:T(128)} %bitcast.17, bf16[4,8192]{1,0:T(4,128)(2,1)} %q_hbm.1, bf16[4,7168]{1,0:T(4,128)(2,1)} %resid_hbm.1, f32[1,7168]{1,0:T(1,128)} %bitcast.15, bf16[4,1024,256]{2,1,0:T(8,128)(2,1)} %k_hbm.1, bf16[4,1024,256]{2,1,0:T(8,128)(2,1)} %v_hbm.1, ...), custom_call_target="tpu_custom_call" | custom-call | tf_op jit(solution)/shard_map/pallas_call | solution.py:620
  81.1 0.6 copy.14

commit v12 on v11

--- a/solution.py
+++ b/solution.py
@@ -344,20 +344,23 @@
     both(steps)
     loads[4].wait()
 
-    def project(plane):
+    def project(plane, arrive):
         def rows(hh, cols):
             return ctx_all[hh, pl.ds(plane * 8, 8), :, cols].reshape(128, 1024)
 
-        def step(i, sums):
+        def first(i, total):
+            cols = pl.ds(pl.multiple_of(i * 1024, 1024), 1024)
+            return total + lax.dot_general(wo[:, cols], rows(0, cols), NT, preferred_element_type=F32)
+
+        def second(i, total):
             cols = pl.ds(pl.multiple_of(i * 1024, 1024), 1024)
             last = pl.ds(pl.multiple_of(i * 1024 + CW // 2, 1024), 1024)
-            one = lax.dot_general(wo[:, cols], rows(0, cols), NT, preferred_element_type=F32)
-            two = lax.dot_general(rows(1, cols), wo[:, last], NT, preferred_element_type=F32)
-            return sums[0] + one, sums[1] + two
-
-        one, two = lax.fori_loop(
-            0, CW // 2048, step, (jnp.zeros((COLS, 128), F32), jnp.zeros((128, COLS), F32))
-        )
+            return total + lax.dot_general(rows(1, cols), wo[:, last], NT, preferred_element_type=F32)
+
+        arrive(0)
+        one = lax.fori_loop(0, CW // 2048, first, jnp.zeros((COLS, 128), F32))
+        arrive(1)
+        two = lax.fori_loop(0, CW // 2048, second, jnp.zeros((128, COLS), F32))
         for zv in range(2):
             for i in range(4):
                 for j in range(4):
@@ -409,11 +412,9 @@
         act = gate / (1.0 + jnp.exp(-gate)) * (acc[i, FH:] * factor)
         return act.T.astype(BF16)
 
-    ht[c, me[0]] = project(c)
+    ht[c, me[0]] = project(c, lambda hh: None)
     next(early)
-    both(steps)
-    both(steps)
-    ht[co, me[1]] = project(co)
+    ht[co, me[1]] = project(co, lambda hh: (next(steps[hh]), next(steps[hh])))
     next(late)
     acc[...] = jnp.zeros_like(acc)
     squares[...] = jnp.zeros_like(squares)
@@ -456,33 +457,37 @@
         rows = other_order() if h else lhs
         ak, (b, b1, b2, b3), a_other, b_other = ways[h]
         a, b_right, b_left = ak[0], b_other[1], b_other[3]
+        def slab(p, k, j):
+            return p_own.at[h, zs[p] * 4 + k, :, pl.ds(j * 1792, 1792)]
+
+        def spot(i, j):
+            return r2.at[h, i, :, pl.ds(j * 1792, 1792)]
+
+        def send(ref, i, j, to):
+            push(ref, spot(i, j), ds_sem, dr_sem, 32 + 12 * h + 6 * j + i, to)
+
+        def wait(i, j):
+            landed(spot(i, j), ds_sem, dr_sem, 32 + 12 * h + 6 * j + i)
+
         for j in range(2):
             cols = pl.ds(j * 1792, 1792)
             part = jnp.dot(rows, wd[:, pl.ds(h * 3584 + j * 1792, 1792)], preferred_element_type=F32)
             p_own[h, :, :, cols] = part.astype(BF16).reshape(8, 16, 1792)
-
-        def slab(p, k):
-            return p_own.at[h, zs[p] * 4 + k]
-
-        def send(ref, i, to):
-            push(ref, r2.at[h, i], ds_sem, dr_sem, 2 + 6 * h + i, to)
-
-        def wait(i):
-            landed(r2.at[h, i], ds_sem, dr_sem, 2 + 6 * h + i)
-
-        send(slab(0, b2), 0, b_left)
-        send(slab(1, b2), 1, b_right)
-        send(slab(1, b3), 3, b_left)
-        send(slab(0, b1), 4, b_right)
-        yield
-        for i, p, k, to, j in ((0, 0, b3, b_left, 2), (1, 1, b1, b_right, 5)):
-            wait(i)
-            ref = slab(p, k)
-            ref[...] = (ref[...].astype(F32) + r2[h, i].astype(F32)).astype(BF16)
-            send(ref, j, to)
-        yield
-        for i in (3, 4, 2, 5):
-            wait(i)
+            send(slab(0, b2, j), 0, j, b_left)
+            send(slab(1, b2, j), 1, j, b_right)
+            send(slab(1, b3, j), 3, j, b_left)
+            send(slab(0, b1, j), 4, j, b_right)
+        yield
+        for j in range(2):
+            for i, p, k, to, n in ((0, 0, b3, b_left, 2), (1, 1, b1, b_right, 5)):
+                wait(i, j)
+                ref = slab(p, k, j)
+                ref[...] = (ref[...].astype(F32) + spot(i, j)[...].astype(F32)).astype(BF16)
+                send(ref, n, j, to)
+        yield
+        for j in range(2):
+            for i in (3, 4, 2, 5):
+                wait(i, j)
         for p in (1, 0):
             total = (
                 p_own[h, zs[p] * 4 + b].astype(F32) + r2[h, 2 + p].astype(F32) + r2[h, 4 + p].astype(F32)
@@ -623,7 +628,7 @@
         in_specs=[smem] * 3 + [hbm] * 9,
         out_specs=vmem,
         scratch_shapes=[pltpu.VMEM(shape, dtype) for shape, dtype in scratch]
-        + [dma((n,)) for n in (8, 7, 42, 42, 42, 42, 32, 32, 26, 26)],
+        + [dma((n,)) for n in (8, 7, 42, 42, 42, 42, 56, 56, 26, 26)],
         compiler_params=pltpu.CompilerParams(
             collective_id=0, has_side_effects=True, vmem_limit_bytes=60 * 1024 * 1024
         ),

time: 81.9 us -> 83.4 us (1.018)
  Pallas kernels: 81.1 us -> 82.6 us
    pallas_call x1, Pallas kernels: 81.1 us -> 82.6 us  [per_device(): pl.pallas_call(kernel, out_shape=pltpu.VMEM((4, D), BF16), in_specs=[smem...]
where the time goes in v12:
time: 83.4 us; the launch traced here: 83.3 us
  Pallas kernels  82.6 us (99%)
    pallas_call x1, Pallas kernels, per_device(): pl.pallas_call(kernel, out_shape=pltpu.VMEM((4, D), BF16), in_specs=[smem...  82.6 us

profile of v12, /device:TPU:0, one launch (start us, length us, event | category | flops | bytes accessed | tf_op | source)
XLA Modules:
  0.0 83.3 jit_solution(18143735527926594166)
XLA Ops:
  0.0 82.6 %shard_map.118 = bf16[4,7168]{1,0:T(4,128)(2,1)S(1)} custom-call(s32[4]{0:T(128)} %len_ref.1, s32[4]{0:T(128)} %bitcast.16, s32[2]{0:T(128)} %bitcast.17, bf16[4,8192]{1,0:T(4,128)(2,1)} %q_hbm.1, bf16[4,7168]{1,0:T(4,128)(2,1)} %resid_hbm.1, f32[1,7168]{1,0:T(1,128)} %bitcast.15, bf16[4,1024,256]{2,1,0:T(8,128)(2,1)} %k_hbm.1, bf16[4,1024,256]{2,1,0:T(8,128)(2,1)} %v_hbm.1, ...), custom_call_target="tpu_custom_call" | custom-call | tf_op jit(solution)/shard_map/pallas_call | solution.py:625
  82.6 0.6 copy.14

commit v13 on v11

--- a/solution.py
+++ b/solution.py
@@ -48,11 +48,12 @@
 
     q_load = pltpu.make_async_copy(q_hbm, q_ref, w_sem.at[6])
     q_load.start()
-    fetch = []
-    for src, dst in ((k_hbm, kc), (v_hbm, vc)):
-        for r in range(4):
-            fetch.append(pltpu.make_async_copy(src.at[r], dst.at[r], kv_sem.at[len(fetch)]))
-            fetch[-1].start()
+    fetch = [
+        pltpu.make_async_copy(src, dst, kv_sem.at[i])
+        for i, (src, dst) in enumerate(((k_hbm, kc), (v_hbm, vc)))
+    ]
+    for copy in fetch:
+        copy.start()
     loads = [
         pltpu.make_async_copy(src, dst, w_sem.at[i])
         for i, (src, dst) in enumerate(
@@ -103,15 +104,13 @@
         expo = jnp.exp(scores - jnp.max(scores, axis=-1, keepdims=True))
         return (expo / jnp.sum(expo, axis=-1, keepdims=True)).astype(BF16)
 
-    for copy in fetch[:4]:
-        copy.wait()
+    fetch[0].wait()
     for load in loads:
         load.start()
     pl.semaphore_wait(barrier, 16)
     push(d_hbm, wd.at[pl.ds(FH, FH)], rs_sem, rr_sem, 18, sibling)
     probs = [weigh(r) for r in range(4)]
-    for copy in fetch[4:]:
-        copy.wait()
+    fetch[1].wait()
     contexts = [jnp.dot(probs[r], vc[r], preferred_element_type=F32) for r in range(4)]
     for p in range(4):
         chosen = contexts[0]
@@ -120,7 +119,7 @@
         for hh in range(2):
             own_b[hh, p * 16 : p * 16 + 16] = chosen[hh * 16 : hh * 16 + 16].astype(BF16)
 
-    def gather(way, block, part, other, s_sem, r_sem, ready, base, peer=None):
+    def gather(way, block, part, pair, other, other_pair, s_sem, r_sem, ready, base, peer=None):
         ak, bk, a_other, b_other = way
         a, (b, b1, b2, b3) = ak[0], bk
         b_right, b_left = b_other[1], b_other[3]
@@ -142,7 +141,6 @@
             first, second = ((7, b_right), (8, b_left)) if p == 0 else ((10, b_left), (9, b_right))
             send(part(p, b), *first)
             send(part(p, b), *second)
-            send(part(p, b), 13 + p, sibling)
 
         if peer is None:
             send(block(0, a), 0, z_peer)
@@ -158,31 +156,31 @@
             ring_2(0)
         yield
         ring_2(1)
+        send(pair(b), 13, sibling)
         yield
         wait(part(0, b3), 7)
         send(part(0, b3), 11, b_right)
-        send(part(0, b3), 15, sibling)
         wait(part(0, b1), 8)
-        send(part(0, b1), 16, sibling)
         yield
         wait(part(1, b1), 10)
         send(part(1, b1), 12, b_left)
-        send(part(1, b1), 17, sibling)
+        send(pair(b1), 15, sibling)
         wait(part(1, b3), 9)
-        send(part(1, b3), 18, sibling)
+        send(pair(b3), 14, sibling)
         yield
         wait(part(0, b2), 11)
-        send(part(0, b2), 19, sibling)
+        send(part(0, b2), 16, sibling)
         wait(part(1, b2), 12)
-        send(part(1, b2), 20, sibling)
-        yield
-        for p, spots in enumerate((((13, 0), (15, 3), (16, 1), (19, 2)), ((14, 0), (18, 3), (17, 1), (20, 2)))):
-            for i, k in spots:
-                wait(other(zs[p], ak[k]), i)
-            yield
+        send(part(1, b2), 17, sibling)
+        yield
+        for i, k in ((13, 0), (15, 1), (14, 3)):
+            wait(other_pair(ak[k]), i)
+        wait(other(z, ak[2]), 16)
+        yield
+        wait(other(zo, ak[2]), 17)
+        yield
 
     a, b = ways[0][0][0], ways[0][1][0]
-    me = (((c * 2 + z) * 4 + b) * 4 + a, ((c * 2 + z) * 4 + a) * 4 + b)
     me_row = ((z * 4 + b) * 4 + a) * 4
 
     def residual():
@@ -271,9 +269,8 @@
     for hh in range(2):
         push(own_b.at[hh], got_b.at[hh], rs_sem, rr_sem, 20 * hh, partner)
     push(flag_out, flag_in, rs_sem, rr_sem, 21, z_peer)
-    for hh in range(2):
-        push(own_b.at[hh], cross_b.at[hh], rs_sem, rr_sem, 22 + hh, cross)
-        push(own_b.at[hh], peer_b.at[hh], rs_sem, rr_sem, 24 + hh, z_peer)
+    push(own_b, cross_b, rs_sem, rr_sem, 22, cross)
+    push(own_b, peer_b, rs_sem, rr_sem, 24, z_peer)
     residual_steps, scaling_steps = residual(), scaling()
     next(residual_steps)
     next(scaling_steps)
@@ -288,7 +285,7 @@
             for h in range(16):
                 for half in range(2):
                     first = h * 256 + half * 128
-                    ctx_all[hh, (c * 2 + zs[p]) * 4 + way[1][0], :, first : first + 128] = sf[
+                    ctx_all[hh, c, zs[p], way[1][0], :, first : first + 128] = sf[
                         half, pl.ds(h, 16, stride=16), :
                     ].astype(BF16)
 
@@ -300,8 +297,8 @@
         def peer():
             if hh == 0:
                 landed(flag_in, rs_sem, rr_sem, 21)
-            landed(cross_b.at[hh], rs_sem, rr_sem, 22 + hh)
-            landed(peer_b.at[hh], rs_sem, rr_sem, 24 + hh)
+                landed(cross_b, rs_sem, rr_sem, 22)
+                landed(peer_b, rs_sem, rr_sem, 24)
             wide = flag_in[...].astype(F32)
             flag = jnp.concatenate(
                 [jnp.broadcast_to(wide[m * 8 : m * 8 + 1], (32, 128)) for m in range(2)], axis=0
@@ -313,8 +310,10 @@
         yield from gather(
             way,
             lambda p, av: cb.at[hh, zs[p], av],
-            lambda p, bv: ctx_all.at[hh, (c * 2 + zs[p]) * 4 + bv],
-            lambda zv, bv: ctx_all.at[hh, (co * 2 + zv) * 4 + bv],
+            lambda p, bv: ctx_all.at[hh, c, zs[p], bv],
+            lambda bv: ctx_all.at[hh, c, :, bv],
+            lambda zv, bv: ctx_all.at[hh, co, zv, bv],
+            lambda bv: ctx_all.at[hh, co, :, bv],
             bs_sem,
             br_sem,
             ready,
@@ -346,7 +345,7 @@
 
     def project(plane):
         def rows(hh, cols):
-            return ctx_all[hh, pl.ds(plane * 8, 8), :, cols].reshape(128, 1024)
+            return ctx_all[hh, plane, :, :, :, cols].reshape(128, 1024)
 
         def step(i, sums):
             cols = pl.ds(pl.multiple_of(i * 1024, 1024), 1024)
@@ -370,9 +369,11 @@
         half = (c, co)[i]
         return gather(
             ways[i],
-            lambda p, av: ht.at[half, ((c * 2 + zs[p]) * 4 + ways[i][1][0]) * 4 + av],
-            lambda p, bv: ht.at[half, pl.ds(((c * 2 + zs[p]) * 4 + bv) * 4, 4)],
-            lambda zv, bv: ht.at[(co, c)[i], pl.ds(((co * 2 + zv) * 4 + bv) * 4, 4)],
+            lambda p, av: ht.at[half, c, zs[p], ways[i][1][0], av],
+            lambda p, bv: ht.at[half, c, zs[p], bv],
+            lambda bv: ht.at[half, c, :, bv],
+            lambda zv, bv: ht.at[(co, c)[i], co, zv, bv],
+            lambda bv: ht.at[(co, c)[i], co, :, bv],
             cs_sem,
             cr_sem,
             lambda p: None,
@@ -387,7 +388,7 @@
             for yv in range(4):
                 xv = n // 2 * 2 + x2
                 bv, av = yv * (1 - half) + xv * half, xv * (1 - half) + yv * half
-                parts.append(ht[half, ((plane * 2 + lax.rem(n, 2)) * 4 + bv) * 4 + av])
+                parts.append(ht[half, plane, lax.rem(n, 2), bv, av])
         return jnp.concatenate(parts, axis=0)
 
     def expand(plane, i, *ps):
@@ -409,11 +410,11 @@
         act = gate / (1.0 + jnp.exp(-gate)) * (acc[i, FH:] * factor)
         return act.T.astype(BF16)
 
-    ht[c, me[0]] = project(c)
+    ht[c, c, z, b, a] = project(c)
     next(early)
     both(steps)
     both(steps)
-    ht[co, me[1]] = project(co)
+    ht[co, c, z, a, b] = project(co)
     next(late)
     acc[...] = jnp.zeros_like(acc)
     squares[...] = jnp.zeros_like(squares)
@@ -491,17 +492,16 @@
                 for q in range(4):
                     qf[av, q * 4 : q * 4 + 4, :] = total[av * 4 : av * 4 + 4, q * 896 : (q + 1) * 896]
             qb[h, p] = qf[...].astype(BF16)
-            for k in (1, 3, 2):
-                push(
-                    qb.at[h, p, ak[k]], r1.at[h, p, k - 1], ds_sem, dr_sem, 13 + 6 * h + 3 * p + k, a_other[k]
-                )
-        yield
+        for k in (1, 3, 2):
+            push(qb.at[h, :, ak[k]], r1.at[h, k - 1], ds_sem, dr_sem, 13 + 6 * h + k, a_other[k])
+        yield
+        for k in (1, 3, 2):
+            landed(r1.at[h, k - 1], ds_sem, dr_sem, 13 + 6 * h + k)
         sums = []
         for p in (1, 0):
             total = qb[h, p, a].astype(F32)
             for k in (1, 3, 2):
-                landed(r1.at[h, p, k - 1], ds_sem, dr_sem, 13 + 6 * h + 3 * p + k)
-                total = total + r1[h, p, k - 1].astype(F32)
+                total = total + r1[h, k - 1, p].astype(F32)
             sums.append(total)
             if p == 1:
                 tz[h] = total.astype(BF16)
@@ -539,12 +539,13 @@
             for yv in range(4):
                 for plane in range(2):
                     bv, av = yv * co + xv * c, xv * co + yv * c
-                    parts.append(ht[c, ((plane * 2 + zv) * 4 + bv) * 4 + av])
+                    parts.append(ht[c, plane, zv, bv, av])
             rows = rows + lax.dot_general(
                 pick, jnp.concatenate(parts, axis=0), NT, preferred_element_type=F32
             )
         hid[h] = rows.astype(BF16)
-        push(hid.at[h], hid_got.at[h], rs_sem, rr_sem, 16 + h, partner)
+        if h:
+            push(hid, hid_got, rs_sem, rr_sem, 16, partner)
 
     halves = (reduction(0), reduction(1))
     before = len(started)
@@ -558,8 +559,7 @@
     for _ in range(2):
         for half in halves:
             next(half)
-    for h in range(2):
-        landed(hid_got.at[h], rs_sem, rr_sem, 16 + h)
+    landed(hid_got, rs_sem, rr_sem, 16)
     for half in halves:
         next(half)
     drain()
@@ -593,8 +593,8 @@
         ((16, 128), BF16),
         ((2, 2, 4, 64, 256), BF16),
         ((2, 256, 128), F32),
-        ((2, 16, 16, CW // 2), BF16),
-        ((2, 64, COLS, 128), BF16),
+        ((2, 2, 2, 4, 16, CW // 2), BF16),
+        ((2, 2, 2, 4, 4, COLS, 128), BF16),
         ((2, 2 * FH, 128), F32),
         ((2, 8, 128), F32),
         ((128, FH), BF16),
@@ -614,7 +614,7 @@
         ((2, 6, 16, D // 2), BF16),
         ((4, 16, 896), F32),
         ((2, 2, 4, 16, 896), BF16),
-        ((2, 2, 3, 16, 896), BF16),
+        ((2, 3, 2, 16, 896), BF16),
         ((2, 16, 896), F32),
     ) + (((2, 16, 896), BF16),) * 7
     return pl.pallas_call(

time: 81.9 us -> 82 us (level)
  no operation moved by 1% of the time
where the time goes in v13:
time: 82 us; the launch traced here: 81.9 us
  Pallas kernels  81.2 us (99%)
    pallas_call x1, Pallas kernels, per_device(): pl.pallas_call(kernel, out_shape=pltpu.VMEM((4, D), BF16), in_specs=[smem...  81.2 us

profile of v13, /device:TPU:0, one launch (start us, length us, event | category | flops | bytes accessed | tf_op | source)
XLA Modules:
  0.0 81.9 jit_solution(15418712127535308883)
XLA Ops:
  0.0 81.2 %shard_map.118 = bf16[4,7168]{1,0:T(4,128)(2,1)S(1)} custom-call(s32[4]{0:T(128)} %len_ref.1, s32[4]{0:T(128)} %bitcast.16, s32[2]{0:T(128)} %bitcast.17, bf16[4,8192]{1,0:T(4,128)(2,1)} %q_hbm.1, bf16[4,7168]{1,0:T(4,128)(2,1)} %resid_hbm.1, f32[1,7168]{1,0:T(1,128)} %bitcast.15, bf16[4,1024,256]{2,1,0:T(8,128)(2,1)} %k_hbm.1, bf16[4,1024,256]{2,1,0:T(8,128)(2,1)} %v_hbm.1, ...), custom_call_target="tpu_custom_call" | custom-call | tf_op jit(solution)/shard_map/pallas_call | solution.py:620
  81.3 0.6 copy.14

commit v14 on v11

--- a/solution.py
+++ b/solution.py
@@ -330,16 +330,16 @@
 
     both(steps)
     next(residual_steps)
-    both(steps)
     next(scaling_steps)
+    both(steps)
     both(steps)
     next(residual_steps)
     next(scaling_steps)
-    both(steps)
     next(scaling_steps)
     both(steps)
+    both(steps)
+    next(residual_steps)
     next(scaling_steps)
-    next(residual_steps)
     next(scaling_steps)
     both(steps)
     loads[4].wait()

time: 81.9 us -> 82.7 us (level)
  Pallas kernels: 81.1 us -> 82 us
    pallas_call x1, Pallas kernels: 81.1 us -> 82 us  [per_device(): pl.pallas_call(kernel, out_shape=pltpu.VMEM((4, D), BF16), in_specs=[smem...]
where the time goes in v14:
time: 82.7 us; the launch traced here: 82.6 us
  Pallas kernels  82 us (99%)
    pallas_call x1, Pallas kernels, per_device(): pl.pallas_call(kernel, out_shape=pltpu.VMEM((4, D), BF16), in_specs=[smem...  82 us

profile of v14, /device:TPU:0, one launch (start us, length us, event | category | flops | bytes accessed | tf_op | source)
XLA Modules:
  0.0 82.6 jit_solution(5372442034076342271)
XLA Ops:
  0.0 82.0 %shard_map.118 = bf16[4,7168]{1,0:T(4,128)(2,1)S(1)} custom-call(s32[4]{0:T(128)} %len_ref.1, s32[4]{0:T(128)} %bitcast.16, s32[2]{0:T(128)} %bitcast.17, bf16[4,8192]{1,0:T(4,128)(2,1)} %q_hbm.1, bf16[4,7168]{1,0:T(4,128)(2,1)} %resid_hbm.1, f32[1,7168]{1,0:T(1,128)} %bitcast.15, bf16[4,1024,256]{2,1,0:T(8,128)(2,1)} %k_hbm.1, bf16[4,1024,256]{2,1,0:T(8,128)(2,1)} %v_hbm.1, ...), custom_call_target="tpu_custom_call" | custom-call | tf_op jit(solution)/shard_map/pallas_call | solution.py:620
  82.0 0.6 copy.14

commit v15 on v11

--- a/solution.py
+++ b/solution.py
@@ -107,8 +107,6 @@
         copy.wait()
     for load in loads:
         load.start()
-    pl.semaphore_wait(barrier, 16)
-    push(d_hbm, wd.at[pl.ds(FH, FH)], rs_sem, rr_sem, 18, sibling)
     probs = [weigh(r) for r in range(4)]
     for copy in fetch[4:]:
         copy.wait()
@@ -119,6 +117,7 @@
             chosen = jnp.where(assign_ref[p] == r, contexts[r], chosen)
         for hh in range(2):
             own_b[hh, p * 16 : p * 16 + 16] = chosen[hh * 16 : hh * 16 + 16].astype(BF16)
+    pl.semaphore_wait(barrier, 16)
 
     def gather(way, block, part, other, s_sem, r_sem, ready, base, peer=None):
         ak, bk, a_other, b_other = way
@@ -274,6 +273,7 @@
     for hh in range(2):
         push(own_b.at[hh], cross_b.at[hh], rs_sem, rr_sem, 22 + hh, cross)
         push(own_b.at[hh], peer_b.at[hh], rs_sem, rr_sem, 24 + hh, z_peer)
+    push(d_hbm, wd.at[pl.ds(FH, FH)], rs_sem, rr_sem, 18, sibling)
     residual_steps, scaling_steps = residual(), scaling()
     next(residual_steps)
     next(scaling_steps)

time: 81.9 us -> 81.6 us (level)
  no operation moved by 1% of the time
where the time goes in v15:
time: 81.6 us; the launch traced here: 81.2 us
  Pallas kernels  80.6 us (99%)
    pallas_call x1, Pallas kernels, per_device(): pl.pallas_call(kernel, out_shape=pltpu.VMEM((4, D), BF16), in_specs=[smem...  80.6 us

profile of v15, /device:TPU:0, one launch (start us, length us, event | category | flops | bytes accessed | tf_op | source)
XLA Modules:
  0.0 81.2 jit_solution(1338668668604289963)
XLA Ops:
  0.0 80.6 %shard_map.118 = bf16[4,7168]{1,0:T(4,128)(2,1)S(1)} custom-call(s32[4]{0:T(128)} %len_ref.1, s32[4]{0:T(128)} %bitcast.16, s32[2]{0:T(128)} %bitcast.17, bf16[4,8192]{1,0:T(4,128)(2,1)} %q_hbm.1, bf16[4,7168]{1,0:T(4,128)(2,1)} %resid_hbm.1, f32[1,7168]{1,0:T(1,128)} %bitcast.15, bf16[4,1024,256]{2,1,0:T(8,128)(2,1)} %k_hbm.1, bf16[4,1024,256]{2,1,0:T(8,128)(2,1)} %v_hbm.1, ...), custom_call_target="tpu_custom_call" | custom-call | tf_op jit(solution)/shard_map/pallas_call | solution.py:620
  80.6 0.6 copy.14

commit v16 on v15

--- a/solution.py
+++ b/solution.py
@@ -491,17 +491,16 @@
                 for q in range(4):
                     qf[av, q * 4 : q * 4 + 4, :] = total[av * 4 : av * 4 + 4, q * 896 : (q + 1) * 896]
             qb[h, p] = qf[...].astype(BF16)
-            for k in (1, 3, 2):
-                push(
-                    qb.at[h, p, ak[k]], r1.at[h, p, k - 1], ds_sem, dr_sem, 13 + 6 * h + 3 * p + k, a_other[k]
-                )
-        yield
+        for k in (1, 3, 2):
+            push(qb.at[h, :, ak[k]], r1.at[h, k - 1], ds_sem, dr_sem, 13 + 6 * h + k, a_other[k])
+        yield
+        for k in (1, 3, 2):
+            landed(r1.at[h, k - 1], ds_sem, dr_sem, 13 + 6 * h + k)
         sums = []
         for p in (1, 0):
             total = qb[h, p, a].astype(F32)
             for k in (1, 3, 2):
-                landed(r1.at[h, p, k - 1], ds_sem, dr_sem, 13 + 6 * h + 3 * p + k)
-                total = total + r1[h, p, k - 1].astype(F32)
+                total = total + r1[h, k - 1, p].astype(F32)
             sums.append(total)
             if p == 1:
                 tz[h] = total.astype(BF16)
@@ -614,7 +613,7 @@
         ((2, 6, 16, D // 2), BF16),
         ((4, 16, 896), F32),
         ((2, 2, 4, 16, 896), BF16),
-        ((2, 2, 3, 16, 896), BF16),
+        ((2, 3, 2, 16, 896), BF16),
         ((2, 16, 896), F32),
     ) + (((2, 16, 896), BF16),) * 7
     return pl.pallas_call(

time: 81.6 us -> 81.8 us (level)
  no operation moved by 1% of the time
where the time goes in v16:
time: 81.8 us; the launch traced here: 81.6 us
  Pallas kernels  81 us (99%)
    pallas_call x1, Pallas kernels, per_device(): pl.pallas_call(kernel, out_shape=pltpu.VMEM((4, D), BF16), in_specs=[smem...  81 us

profile of v16, /device:TPU:0, one launch (start us, length us, event | category | flops | bytes accessed | tf_op | source)
XLA Modules:
  0.0 81.6 jit_solution(17562405566968837361)
XLA Ops:
  0.0 81.0 %shard_map.118 = bf16[4,7168]{1,0:T(4,128)(2,1)S(1)} custom-call(s32[4]{0:T(128)} %len_ref.1, s32[4]{0:T(128)} %bitcast.16, s32[2]{0:T(128)} %bitcast.17, bf16[4,8192]{1,0:T(4,128)(2,1)} %q_hbm.1, bf16[4,7168]{1,0:T(4,128)(2,1)} %resid_hbm.1, f32[1,7168]{1,0:T(1,128)} %bitcast.15, bf16[4,1024,256]{2,1,0:T(8,128)(2,1)} %k_hbm.1, bf16[4,1024,256]{2,1,0:T(8,128)(2,1)} %v_hbm.1, ...), custom_call_target="tpu_custom_call" | custom-call | tf_op jit(solution)/shard_map/pallas_call | solution.py:619
  81.0 0.6 copy.14
